TPU v7x, 32 devices: a whole 2x2x4 slice. The times are simulated.
32 devices in a mesh: dom: 8 (over z, x), bucket: 2 (over core), depth: 2 (over y).
Axes of the slice: x: 2, y: 2, z: 4, core: 2. Of those that a mesh axis runs over, the one named last changes fastest.
Arguments:
- entities: float32 [16384, 400], P(('dom', 'bucket')), may hold values from -7 to 7
- entity_state: float32 [16384], P(('dom', 'bucket')), may hold values from 0.05 to 0.5
- relations: float32 [256, 400], replicated, may hold values from 0.5 to 2
- relation_state: float32 [256], replicated, may hold values from 0.05 to 0.5
- edge_ends: int32 [2, 16384], P(None, ('dom', 'bucket')), may hold values from 0 to 1023
- relation_ids: int32 [16384], P(('dom', 'bucket')), may hold values from 0 to 255
- neg_ids: int32 [32, 1024], P(('dom', 'bucket'), 'depth'), may hold values from 0 to 1023
- edge_count: int32 [16], P(('dom', 'bucket')), may hold values from 16 to 1024, as said below
Outputs:
- new_entities: float32 [16384, 400], P(('dom', 'bucket'))
- new_state: float32 [16384], P(('dom', 'bucket'))
- new_relations: float32 [256, 400], replicated
Inputs may be any that keep to these rules, and one draw needn't show every extreme that they name: `edge_count`: the live slots of a partition are its first ones; partition 0 is full in every draw.
All inputs are finite; a program needn't handle non-finite values.
Results may differ from a plain program's by a relative error of at most 0.0006.
The roundings to bfloat16 on the way count: a program that leaves them out, or rounds other values in their place, can miss the bound.
Values may be sent and summed in bfloat16 or wider, within the bound.
A program may use at most 64 MiB of HBM per device.

v0:
```python
import jax
import jax.numpy as jnp
from jax import lax
from jax.sharding import PartitionSpec as P

BLOCK = 512


entity_rate = 0.1
relation_rate = 1.0


def passed_along(block, axis, distance):
    devices = range(lax.axis_size(axis))
    route = [((i - distance) % len(devices), i) for i in devices]
    return lax.ppermute(block, axis, route)


def merged(value, axis, join):
    pieces = jax.tree.map(lambda part: lax.all_gather(part, axis), value)
    head = jax.tree.map(lambda part: part[0], pieces)
    tail = jax.tree.map(lambda part: part[1:], pieces)
    total, _ = lax.scan(lambda total, share: (join(total, share), None), head, tail)
    return total


def merge_totals(earlier, later):
    peak = jnp.maximum(earlier[0], later[0])
    return (peak, earlier[1] * jnp.exp(earlier[0] - peak) + later[1] * jnp.exp(later[0] - peak))


def adagrad_rows(values, state, grad):
    updated = state + jnp.mean(grad * grad, axis=1)
    return (values - entity_rate * grad / jnp.sqrt(updated)[:, None], updated)


def pick_rows(table, row_ids):
    columns = jnp.arange(table.shape[0], dtype=jnp.int32)
    selector = (row_ids[:, None] == columns[None, :]).astype(jnp.bfloat16)
    return jnp.dot(selector, table, preferred_element_type=jnp.float32).astype(jnp.bfloat16)


def local(
    entities, entity_state, relations, relation_state, edge_ends, relation_ids, neg_ids, edge_count
):
    half_dom = lax.axis_size("dom") // 2
    row_count = entities.shape[0]
    own_rows = entities.astype(jnp.bfloat16)
    far_rows = passed_along(own_rows, "dom", half_dom)
    live_count = edge_count[0]
    offsets = jnp.arange(BLOCK, dtype=jnp.int32)

    def block_inputs(block_index):
        first_slot = (block_index * BLOCK).astype(jnp.int32)
        left_ids = lax.dynamic_slice_in_dim(edge_ends[0], first_slot, BLOCK)
        right_ids = lax.dynamic_slice_in_dim(edge_ends[1], first_slot, BLOCK)
        rel_ids = lax.dynamic_slice_in_dim(relation_ids, first_slot, BLOCK)
        negative_ids = lax.dynamic_index_in_dim(neg_ids, block_index, 0, keepdims=False)
        active = (first_slot + offsets < live_count).astype(jnp.float32)
        return (first_slot, left_ids, right_ids, rel_ids, negative_ids, active)

    def score_part(left_ids, right_ids, rel_ids, negative_ids):
        left_rows = pick_rows(own_rows, left_ids)
        right_rows = pick_rows(far_rows, right_ids)
        scaling = relations[rel_ids]
        queries = (left_rows.astype(jnp.float32) * scaling).astype(jnp.bfloat16)
        negatives = pick_rows(far_rows, negative_ids)
        positive = jnp.sum(queries.astype(jnp.float32) * right_rows.astype(jnp.float32), axis=1)
        scores = lax.dot_general(
            queries, negatives, (((1,), (1,)), ((), ())), preferred_element_type=jnp.float32
        )
        local_peak = jnp.max(scores, axis=1)
        shifted = jnp.exp(scores - local_peak[:, None])
        local_total = jnp.sum(shifted, axis=1)
        return (
            left_rows,
            right_rows,
            scaling,
            queries,
            negatives,
            positive,
            shifted,
            local_peak,
            local_total,
        )

    def grad_part(
        totals_in, parts, neg_peak, neg_total, left_ids, right_ids, rel_ids, negative_ids, active
    ):
        own_grad, far_grad, rel_grad = totals_in
        (
            left_rows,
            right_rows,
            scaling,
            queries,
            negatives,
            positive,
            shifted,
            local_peak,
            local_total,
        ) = parts
        peak = jnp.maximum(positive, neg_peak)
        denom = jnp.exp(positive - peak) + neg_total * jnp.exp(neg_peak - peak)
        weights = (shifted * (jnp.exp(local_peak - peak) * active / denom)[:, None]).astype(
            jnp.bfloat16
        )
        pos_coef = active * (jnp.exp(positive - peak) / denom - 1.0)
        half_coef = 0.5 * pos_coef
        query_grad = jnp.dot(weights, negatives, preferred_element_type=jnp.float32) + half_coef[
            :, None
        ] * right_rows.astype(jnp.float32)
        neg_grad = lax.dot_general(
            weights, queries, (((0,), (0,)), ((), ())), preferred_element_type=jnp.float32
        )
        own_grad = own_grad.at[left_ids].add(query_grad * scaling)
        far_grad = (
            far_grad.at[right_ids]
            .add(half_coef[:, None] * queries.astype(jnp.float32))
            .at[negative_ids]
            .add(neg_grad)
        )
        rel_grad = rel_grad.at[rel_ids].add(query_grad * left_rows.astype(jnp.float32))
        return (own_grad, far_grad, rel_grad)

    def one_block(block_index, totals_in):
        first_slot, left_ids, right_ids, rel_ids, negative_ids, active = block_inputs(block_index)
        parts = score_part(left_ids, right_ids, rel_ids, negative_ids)
        neg_peak, neg_total = merged((parts[7], parts[8]), "depth", merge_totals)
        return grad_part(
            totals_in,
            parts,
            neg_peak,
            neg_total,
            left_ids,
            right_ids,
            rel_ids,
            negative_ids,
            active,
        )

    zeros_rows = jnp.zeros(entities.shape, jnp.float32)
    start_totals = (zeros_rows, zeros_rows, jnp.zeros(relations.shape, jnp.float32))
    own_grad, far_grad, rel_grad = lax.fori_loop(0, neg_ids.shape[0], one_block, start_totals)
    rel_total = lax.psum(rel_grad, ("dom", "bucket", "depth"))
    rel_state = relation_state + jnp.mean(rel_total * rel_total, axis=1)
    new_relations = relations - relation_rate * rel_total / jnp.sqrt(rel_state)[:, None]
    own_share, far_share = (
        lax.psum_scatter(own_grad, "depth", scatter_dimension=0, tiled=True),
        lax.psum_scatter(far_grad, "depth", scatter_dimension=0, tiled=True),
    )
    home_grad = passed_along(far_share, "dom", half_dom)
    share_rows = row_count // lax.axis_size("depth")
    first_row = lax.axis_index("depth") * share_rows
    values_share = lax.dynamic_slice_in_dim(entities, first_row, share_rows)
    state_share = lax.dynamic_slice_in_dim(entity_state, first_row, share_rows)
    new_values, new_sums = adagrad_rows(values_share, state_share, own_share + home_grad)
    new_entities, new_state = (
        lax.all_gather(new_values, "depth", axis=0, tiled=True),
        lax.all_gather(new_sums, "depth", axis=0, tiled=True),
    )
    return (new_entities, new_state, new_relations)


def solution(mesh):
    return jax.shard_map(
        local,
        mesh=mesh,
        in_specs=(
            P(("dom", "bucket"), None),
            P(("dom", "bucket")),
            P(),
            P(),
            P(None, ("dom", "bucket")),
            P(("dom", "bucket")),
            P(("dom", "bucket"), "depth"),
            P(("dom", "bucket")),
        ),
        out_specs=(P(("dom", "bucket"), None), P(("dom", "bucket")), P()),
        check_vma=False,
    )
```

profile of v0, /device:TPU:24, one launch (start us, length us, event | category | flops | bytes accessed | tf_op | source)
XLA Modules:
  0.0 363.9 jit_solution(11885514043083211292)
XLA Ops:
  11.5 36.5 %collective-permute-done = bf16[1024,400]{0,1:T(8,128)(2,1)S(1)} collective-permute-done((bf16[1024,400]{0,1:T(8,128)(2,1)S(1)}, bf16[1024,400]{0,1:T(8,128)(2,1)S(1)}, u32[]{:S(2)}, u32[]{:S(2)}) %collective-permute-start) | collective-permute-done | bytes 819232 | tf_op jit(solution)/shard_map/ppermute | solution.py:16
  51.3 118.0 %while.31 = (s32[]{:T(128)}, f32[1024,400]{1,0:T(8,128)}, f32[1024,400]{1,0:T(8,128)S(1)}, f32[256,400]{1,0:T(8,128)S(1)}, s32[2,1024]{1,0:T(2,128)S(1)}, /*inde...) while((s32[]{:T(128)}, f32[1024,400]{1,0:T(8,128)}, ...), condition=%wide.region_8.9_spmd.clone, body=%wide.region_0.8_spmd.clone.sunk | while | flops 1895480832 | bytes 50795024 | solution.py:143
  51.9 2.9 fusion.55
  58.5 2.4 copy.46
  61.0 2.6 fusion.56
  65.6 4.3 %all-gather.9 = f32[2,1,512]{2,1,0:T(1,128)S(1)} all-gather(f32[1,1,512]{2,1,0:T(1,128)S(1)} %bitcast.70), channel_id=2, replica_groups=mesh['dom'=8,'bucket'=2,'depth'=2] {'depth'}, dimensions={0}, use_global_device_ids=true | all-gather | bytes 6144 | tf_op jit(solution)/shard_map/while/body/eval_jaxpr/all_gather | solution.py:20
  70.1 4.3 %all-gather.10 = f32[2,1,512]{2,1,0:T(1,128)S(1)} all-gather(f32[1,1,512]{2,1,0:T(1,128)S(1)} %bitcast.74), channel_id=3, replica_groups=mesh['dom'=8,'bucket'=2,'depth'=2] {'depth'}, dimensions={0}, use_global_device_ids=true | all-gather | bytes 6144 | tf_op jit(solution)/shard_map/while/body/eval_jaxpr/all_gather | solution.py:20
  76.9 2.4 copy.47
  79.3 7.1 %scatter_fusion = f32[1024,400]{1,0:T(8,128)} fusion(f32[1024,400]{1,0:T(8,128)} %get-tuple-element.549, s32[512]{0:T(512)} %bitcast.72, f32[512,400]{1,0:T(8,128)} %copy.47), kind=kCustom, calls=%fused_computation.1.clone.clone.1 | custom fusion | flops 204800 | bytes 2459648 | tf_op jit(solution)/shard_map/while/body/eval_jaxpr/scatter-add | solution.py:115
  90.6 5.0 %scatter_fusion.1 = f32[1024,400]{1,0:T(8,128)S(1)} fusion(f32[1024,400]{1,0:T(8,128)S(1)} %get-tuple-element.550, s32[512]{0:T(512)} %bitcast.71, f32[512,400]{1,0:T(8,128)} %copy.48), kind=kCustom, calls=%fused_computation.2.clone.clone.1 | custom fusion | flops 204800 | bytes 2459648 | tf_op jit(solution)/shard_map/while/body/eval_jaxpr/scatter-add | solution.py:118
  95.6 2.7 fusion.63
  98.3 5.0 %scatter_fusion.2 = f32[1024,400]{1,0:T(8,128)S(1)} fusion(f32[1024,400]{1,0:T(8,128)S(1)} %scatter_fusion.1, s32[512]{0:T(512)} %bitcast.75, f32[512,400]{1,0:T(8,128)} %fusion.63), kind=kCustom, calls=%fused_computation.3.clone.clone.1 | custom fusion | flops 204800 | bytes 2459648 | tf_op jit(solution)/shard_map/while/body/eval_jaxpr/scatter-add | solution.py:120
  103.3 2.5 copy.49
  105.8 4.5 %scatter_fusion.3 = f32[256,400]{1,0:T(8,128)S(1)} fusion(f32[256,400]{1,0:T(8,128)S(1)} %get-tuple-element.551, s32[512]{0:T(512)S(1)} %copy-done.12, f32[512,400]{1,0:T(8,128)} %copy.49), kind=kCustom, calls=%fused_computation.4.clone.clone.1 | custom fusion | flops 204800 | bytes 2459648 | tf_op jit(solution)/shard_map/while/body/eval_jaxpr/scatter-add | solution.py:122
  110.9 2.9 fusion.55
  117.5 2.4 copy.46
  120.0 2.6 fusion.56
  124.6 4.3 %all-gather.9 = f32[2,1,512]{2,1,0:T(1,128)S(1)} all-gather(f32[1,1,512]{2,1,0:T(1,128)S(1)} %bitcast.70), channel_id=2, replica_groups=mesh['dom'=8,'bucket'=2,'depth'=2] {'depth'}, dimensions={0}, use_global_device_ids=true | all-gather | bytes 6144 | tf_op jit(solution)/shard_map/while/body/eval_jaxpr/all_gather | solution.py:20
  129.1 4.3 %all-gather.10 = f32[2,1,512]{2,1,0:T(1,128)S(1)} all-gather(f32[1,1,512]{2,1,0:T(1,128)S(1)} %bitcast.74), channel_id=3, replica_groups=mesh['dom'=8,'bucket'=2,'depth'=2] {'depth'}, dimensions={0}, use_global_device_ids=true | all-gather | bytes 6144 | tf_op jit(solution)/shard_map/while/body/eval_jaxpr/all_gather | solution.py:20
  138.3 7.1 %scatter_fusion = f32[1024,400]{1,0:T(8,128)} fusion(f32[1024,400]{1,0:T(8,128)} %get-tuple-element.549, s32[512]{0:T(512)} %bitcast.72, f32[512,400]{1,0:T(8,128)} %copy.47), kind=kCustom, calls=%fused_computation.1.clone.clone.1 | custom fusion | flops 204800 | bytes 2459648 | tf_op jit(solution)/shard_map/while/body/eval_jaxpr/scatter-add | solution.py:115
  149.6 5.0 %scatter_fusion.1 = f32[1024,400]{1,0:T(8,128)S(1)} fusion(f32[1024,400]{1,0:T(8,128)S(1)} %get-tuple-element.550, s32[512]{0:T(512)} %bitcast.71, f32[512,400]{1,0:T(8,128)} %copy.48), kind=kCustom, calls=%fused_computation.2.clone.clone.1 | custom fusion | flops 204800 | bytes 2459648 | tf_op jit(solution)/shard_map/while/body/eval_jaxpr/scatter-add | solution.py:118
  154.7 2.7 fusion.63
  157.3 5.0 %scatter_fusion.2 = f32[1024,400]{1,0:T(8,128)S(1)} fusion(f32[1024,400]{1,0:T(8,128)S(1)} %scatter_fusion.1, s32[512]{0:T(512)} %bitcast.75, f32[512,400]{1,0:T(8,128)} %fusion.63), kind=kCustom, calls=%fused_computation.3.clone.clone.1 | custom fusion | flops 204800 | bytes 2459648 | tf_op jit(solution)/shard_map/while/body/eval_jaxpr/scatter-add | solution.py:120
  162.4 2.5 copy.49
  164.8 4.5 %scatter_fusion.3 = f32[256,400]{1,0:T(8,128)S(1)} fusion(f32[256,400]{1,0:T(8,128)S(1)} %get-tuple-element.551, s32[512]{0:T(512)S(1)} %copy-done.12, f32[512,400]{1,0:T(8,128)} %copy.49), kind=kCustom, calls=%fused_computation.4.clone.clone.1 | custom fusion | flops 204800 | bytes 2459648 | tf_op jit(solution)/shard_map/while/body/eval_jaxpr/scatter-add | solution.py:122
  171.1 2.7 copy.38
  174.0 25.1 %reduce-scatter.5.cloned.1.call-done = f32[512,400]{0,1:T(8,128)} async-done(((f32[1024,400]{0,1:T(8,128)}), f32[512,400]{0,1:T(8,128)}) %reduce-scatter.5.cloned.1.call-update) | async-done | bytes 819216 | tf_op jit(solution)/shard_map/reduce_scatter | solution.py:149
  200.5 28.4 %reduce-scatter.3.cloned.1.call-done = f32[512,400]{0,1:T(8,128)} async-done(((f32[1024,400]{0,1:T(8,128)}), f32[512,400]{0,1:T(8,128)}) %reduce-scatter.3.cloned.1.call-update) | async-done | bytes 819216 | tf_op jit(solution)/shard_map/reduce_scatter | solution.py:148
  229.0 10.9 %collective-permute-done.1 = f32[512,400]{0,1:T(8,128)} collective-permute-done((f32[512,400]{0,1:T(8,128)}, f32[512,400]{0,1:T(8,128)}, u32[]{:S(2)}, u32[]{:S(2)}) %collective-permute-start.1) | collective-permute-done | bytes 819232 | tf_op jit(solution)/shard_map/ppermute | solution.py:16
  244.0 102.2 %all-reduce.2.cloned.1.call-done = f32[256,400]{0,1:T(8,128)} async-done(((f32[256,400]{0,1:T(8,128)}), f32[256,400]{0,1:T(8,128)}) %all-reduce.2.cloned.1.call-update) | async-done | bytes 409616 | tf_op jit(solution)/shard_map/psum | solution.py:144
  349.1 4.3 %all-gather.4 = f32[2,1,512]{2,1,0:T(1,128)S(1)} all-gather(f32[1,1,512]{2,1,0:T(1,128)S(1)} %bitcast.83), channel_id=1, replica_groups=mesh['dom'=8,'bucket'=2,'depth'=2] {'depth'}, dimensions={0}, use_global_device_ids=true | all-gather | bytes 6144 | tf_op jit(solution)/shard_map/all_gather | solution.py:159
  353.4 2.8 copy.69
  (116 shorter events, 45.9 us)
Async XLA Ops:
  8.0 3.4 copy-start.7
  8.0 191.0 %reduce-scatter.5.cloned.1.call-start = ((), (), s32[]{:S(2)}) async-start(), calls=%async_computation.3 | async-start | bytes 2457600 | tf_op jit(solution)/shard_map/reduce_scatter | solution.py:149
  9.7 38.4 %collective-permute-start = (bf16[1024,400]{0,1:T(8,128)(2,1)S(1)}, bf16[1024,400]{0,1:T(8,128)(2,1)S(1)}, u32[]{:S(2)}, u32[]{:S(2)}) collective-permute-start(bf16[1024,400]{0,1:T(8,128)(2,1)S(1)} %convert_element_type.98), channel_id=1, source_target_pairs={{16,0},{20,4},{24,8},{28,12},{0,16},{4,20},{8,24},{12,28},{17,1},{... | collective-permute-start | bytes 2457608 | tf_op jit(solution)/shard_map/ppermute | solution.py:16
  49.3 1.9 copy-start.13
  61.0 2.6 copy-start.15
  61.0 3.2 copy-start.3
  65.0 10.1 %copy-start.1 = (f32[512,400]{0,1:T(8,128)S(1)}, f32[512,400]{0,1:T(8,128)}, u32[]{:S(2)}) copy-start(f32[512,400]{0,1:T(8,128)} %copy.46) | copy-start | bytes 2457604 | tf_op jit(solution)/shard_map/while
  65.0 10.1 %copy-start.2 = (f32[512,400]{0,1:T(8,128)S(1)}, f32[512,400]{0,1:T(8,128)}, u32[]{:S(2)}) copy-start(f32[512,400]{0,1:T(8,128)} %fusion.55) | copy-start | bytes 2457604 | tf_op jit(solution)/shard_map/while
  65.5 11.3 %copy-start = (f32[512,512]{0,1:T(8,128)}, f32[512,512]{0,1:T(8,128)S(1)}, u32[]{:S(2)}) copy-start(f32[512,512]{0,1:T(8,128)S(1)} %get-tuple-element.524) | copy-start | bytes 3145732 | tf_op jit(solution)/shard_map/while
  65.5 11.3 %copy-start.6 = (f32[512]{0:T(512)}, f32[512]{0:T(512)S(1)}, u32[]{:S(2)}) copy-start(f32[512]{0:T(512)S(1)} %get-tuple-element.520) | copy-start | bytes 6148 | tf_op jit(solution)/shard_map/while
  75.1 1.8 copy-start.9
  75.1 1.8 copy-start.10
  98.3 7.5 %copy-start.12 = (s32[512]{0:T(512)S(1)}, s32[512]{0:T(512)}, u32[]{:S(2)}) copy-start(s32[512]{0:T(512)} %copy-done.11) | copy-start | bytes 6148 | tf_op jit(solution)/shard_map/while
  105.8 4.5 %copy-start.14 = (s32[2,1024]{1,0:T(2,128)S(1)}, s32[2,1024]{1,0:T(2,128)}, u32[]{:S(2)}) copy-start(s32[2,1024]{1,0:T(2,128)} %get-tuple-element.616) | copy-start | bytes 24580 | tf_op jit(solution)/shard_map/while
  120.0 2.6 copy-start.15
  120.0 3.2 copy-start.3
  124.0 10.1 %copy-start.1 = (f32[512,400]{0,1:T(8,128)S(1)}, f32[512,400]{0,1:T(8,128)}, u32[]{:S(2)}) copy-start(f32[512,400]{0,1:T(8,128)} %copy.46) | copy-start | bytes 2457604 | tf_op jit(solution)/shard_map/while
  124.0 10.1 %copy-start.2 = (f32[512,400]{0,1:T(8,128)S(1)}, f32[512,400]{0,1:T(8,128)}, u32[]{:S(2)}) copy-start(f32[512,400]{0,1:T(8,128)} %fusion.55) | copy-start | bytes 2457604 | tf_op jit(solution)/shard_map/while
  124.5 11.3 %copy-start = (f32[512,512]{0,1:T(8,128)}, f32[512,512]{0,1:T(8,128)S(1)}, u32[]{:S(2)}) copy-start(f32[512,512]{0,1:T(8,128)S(1)} %get-tuple-element.524) | copy-start | bytes 3145732 | tf_op jit(solution)/shard_map/while
  124.6 11.3 %copy-start.6 = (f32[512]{0:T(512)}, f32[512]{0:T(512)S(1)}, u32[]{:S(2)}) copy-start(f32[512]{0:T(512)S(1)} %get-tuple-element.520) | copy-start | bytes 6148 | tf_op jit(solution)/shard_map/while
  134.1 1.8 copy-start.9
  157.3 7.5 %copy-start.12 = (s32[512]{0:T(512)S(1)}, s32[512]{0:T(512)}, u32[]{:S(2)}) copy-start(s32[512]{0:T(512)} %copy-done.11) | copy-start | bytes 6148 | tf_op jit(solution)/shard_map/while
  164.8 4.5 %copy-start.14 = (s32[2,1024]{1,0:T(2,128)S(1)}, s32[2,1024]{1,0:T(2,128)}, u32[]{:S(2)}) copy-start(s32[2,1024]{1,0:T(2,128)} %get-tuple-element.616) | copy-start | bytes 24580 | tf_op jit(solution)/shard_map/while
  171.1 57.9 %reduce-scatter.3.cloned.1.call-start = ((), (), s32[]{:S(2)}) async-start(), calls=%async_computation.2 | async-start | bytes 2457600 | tf_op jit(solution)/shard_map/reduce_scatter | solution.py:148
  173.9 67.6 %copy-start.16 = (f32[1024]{0:T(1024)S(1)}, f32[1024]{0:T(1024)}, u32[]{:S(2)}) copy-start(f32[1024]{0:T(1024)} %param.11) | copy-start | bytes 12292
  173.9 67.6 %copy-start.4 = (f32[1024,400]{0,1:T(8,128)S(1)}, f32[1024,400]{0,1:T(8,128)}, u32[]{:S(2)}) copy-start(f32[1024,400]{0,1:T(8,128)} %param.10) | copy-start | bytes 4915204
  173.9 172.3 %all-reduce.2.cloned.1.call-start = ((), (), s32[]{:S(2)}) async-start(), calls=%async_computation.5 | async-start | bytes 819200 | tf_op jit(solution)/shard_map/psum | solution.py:144
  199.0 40.9 %collective-permute-start.1 = (f32[512,400]{0,1:T(8,128)}, f32[512,400]{0,1:T(8,128)}, u32[]{:S(2)}, u32[]{:S(2)}) collective-permute-start(f32[512,400]{0,1:T(8,128)} %reduce-scatter.5.cloned.1.call-done), channel_id=1, source_target_pairs={{16,0},{20,4},{24,8},{28,12},{0,16},{4,20},{8,24},{12,28},{17,1},{... | collective-permute-start | bytes 2457608 | tf_op jit(solution)/shard_map/ppermute | solution.py:16
  200.5 152.9 %all-gather.13.cloned.1.call-start = ((), (), s32[]{:S(2)}) async-start(), calls=%async_computation.4 | async-start | bytes 2457600 | tf_op jit(solution)/shard_map/all_gather | solution.py:158
  229.0 12.6 %copy-start.5 = (f32[512,400]{0,1:T(8,128)S(1)}, f32[512,400]{0,1:T(8,128)}, u32[]{:S(2)}) copy-start(f32[512,400]{0,1:T(8,128)} %reduce-scatter.3.cloned.1.call-done) | copy-start | bytes 2457604
  241.5 105.7 %copy-start.17 = (f32[256]{0:T(256)S(1)}, f32[256]{0:T(256)}, u32[]{:S(2)}) copy-start(f32[256]{0:T(256)} %param.13) | copy-start | bytes 3076
  241.5 105.7 %copy-start.8 = (f32[256,400]{0,1:T(8,128)S(1)}, f32[256,400]{0,1:T(8,128)}, u32[]{:S(2)}) copy-start(f32[256,400]{0,1:T(8,128)} %param.12) | copy-start | bytes 1228804
  (3 other events, 2.9 us)
Sparse Core Ops, SparseCore 0:
  171.2 27.7 reduce-scatter.4
  201.9 26.9 reduce-scatter.2
  244.1 28.0 all-gather.12
Sparse Core Ops, SparseCore 1:
  200.6 145.6 all-reduce.1
where the time goes:
time: 366 us; the launch traced here: 364 us
  waiting for transfers between devices  203 us (55%)
  other arithmetic  60.8 us (17%)
  local copies, waits for them, and re-layouts  39 us (11%)
  matrix products  22.5 us (6%)
  blocking collectives  21.7 us (6%)
  between operations  15.3 us (4%)
    psum x1, waiting for transfers between devices, local(): rel_total = lax.psum(rel_grad, ('dom', 'bucket', 'depth'))  102 us
    ppermute x2, waiting for transfers between devices, passed_along(): return lax.ppermute(block, axis, route)  47.4 us
    reduce_scatter x1, waiting for transfers between devices, local(): lax.psum_scatter(own_grad, 'depth', scatter_dimension=0, tiled=True)  28.4 us
    reduce_scatter x1, waiting for transfers between devices, local(): lax.psum_scatter(far_grad, 'depth', scatter_dimension=0, tiled=True)  25.1 us
    scatter-add x4, other arithmetic, grad_part(): far_grad = far_grad.at[right_ids].add(half_coef[:, None] * queries.astype...  20.1 us
    all_gather x4, blocking collectives, merged(): pieces = jax.tree.map(lambda part: lax.all_gather(part, axis), value)  17.3 us
    scatter-add x2, other arithmetic, grad_part(): own_grad = own_grad.at[left_ids].add(query_grad * scaling)  14.3 us
    dot_general x6, matrix products, pick_rows(): jnp.dot(selector, table, preferred_element_type=jnp.float32)  12.7 us
  transfers between devices with their start and end apart: 6, of which 5 were waited for; matrix products, arithmetic and copies ran while one was open for 3% of the time, Pallas kernels for 0%

commit v1 on v0

v1 whole, which is shorter than its diff:
```python
import functools

import jax
import jax.numpy as jnp
from jax import lax
from jax.experimental import pallas as pl
from jax.experimental.pallas import tpu as pltpu
from jax.sharding import PartitionSpec as P

entity_rate = 0.1
relation_rate = 1.0
MESH = pl.DeviceIdType.MESH
f32, bf16 = jnp.float32, jnp.bfloat16


def dot(a, b):
    return jnp.dot(a, b, preferred_element_type=f32)


def dot_nt(a, b):
    return lax.dot_general(a, b, (((1,), (1,)), ((), ())), preferred_element_type=f32)


def dot_tn(a, b):
    return lax.dot_general(a, b, (((0,), (0,)), ((), ())), preferred_element_type=f32)


def parts_of(value, terms):
    out = []
    for _ in range(terms):
        out.append(value.astype(bf16))
        value = value - out[-1].astype(f32)
    return out


def kernel(
    n_dom,
    block,
    tile,
    ent,
    info_in,
    state_in,
    rel,
    ent_out,
    state_out,
    rg_out,
    left_tab,
    far_tab,
    stage,
    info,
    far_grad,
    own_grad,
    fgb,
    from_mate,
    both,
    from_y,
    fin_send,
    fin,
    ssem,
    rsem,
):
    rows, width = ent.shape
    nrel = rel.shape[0]
    half_rows = rows // 2
    d, b, y = lax.axis_index("dom"), lax.axis_index("bucket"), lax.axis_index("depth")
    half = n_dom // 2
    d2 = lax.rem(d + half, n_dom)
    odd = lax.rem(b, 2)
    b2 = b + 1 - 2 * odd
    y2 = 1 - y
    home = odd == d // half
    away = odd != d // half
    partner, mate, ypeer = (d2, b, y), (d, b2, y), (d, b, y2)
    diag, diag2 = (d2, b2, y), (d2, b2, y2)
    mine = pl.ds(pl.multiple_of(y * half_rows, half_rows), half_rows)
    other = pl.ds(pl.multiple_of(y2 * half_rows, half_rows), half_rows)

    def copy(k, src, dst, device):
        return pltpu.make_async_remote_copy(
            src_ref=src,
            dst_ref=dst,
            send_sem=ssem.at[k],
            recv_sem=rsem.at[k],
            device_id=device,
            device_id_type=MESH,
        )

    barrier = pltpu.get_barrier_semaphore()
    for device in (partner, mate, ypeer, diag, diag2):
        pl.semaphore_signal(barrier, inc=1, device_id=device, device_id_type=MESH)
    pl.semaphore_wait(barrier, 5)

    c_stage = copy(0, stage, far_tab.at[mine], partner)
    c_left = copy(1, left_tab, far_tab, mate)
    c_cross = copy(2, far_tab.at[mine], far_tab.at[mine], ypeer)
    c_cross_in = copy(2, far_tab.at[other], far_tab.at[other], ypeer)
    c_mate0 = copy(3, far_tab.at[mine], left_tab.at[mine], mate)
    c_mate1 = copy(4, far_tab.at[other], left_tab.at[other], mate)
    c_info_home = copy(5, info_in, info.at[1], ypeer)
    c_info_away2 = copy(5, info_in, info.at[1], diag2)
    c_info_away = copy(6, info_in, info.at[0], diag)

    @pl.when(away)
    def _():
        stage[...] = ent[mine, :].astype(bf16)
        c_stage.start()
        c_info_away.start()
        c_info_away2.start()
        c_info_away.wait()
        c_info_away2.wait()

    @pl.when(home)
    def _():
        left_tab[...] = ent[...].astype(bf16)
        c_left.start()
        c_info_home.start()
        info[0] = info_in[...]
        c_info_home.wait()

    columns = jnp.concatenate([info[0], info[1]], axis=0).T
    lane_rows = lax.broadcasted_iota(jnp.int32, (1, rows), 1)
    at_zero = y == 0
    counts = jnp.zeros((1, rows), f32)
    for slot in range(2):
        both_blocks = columns[:, 8 * slot + 4 : 8 * slot + 5]
        ids = jnp.where(at_zero, both_blocks[:half_rows], both_blocks[half_rows:])
        counts += jnp.sum((ids == lane_rows).astype(f32), axis=0, keepdims=True)
    edge_cols = jnp.where(at_zero, columns[:block], columns[block:])

    @pl.when(home)
    def _():
        c_stage.wait_recv()
        c_cross.start()
        c_mate0.start()
        c_cross_in.wait_recv()
        c_mate1.start()

    @pl.when(away)
    def _():
        c_left.wait_recv()
        c_mate0.wait_recv()
        c_mate1.wait_recv()

    rel_terms = parts_of(rel[...], 3)
    lane_rel = lax.broadcasted_iota(jnp.int32, (1, nrel), 1)
    for t in range(block // tile):
        cols = edge_cols[t * tile : (t + 1) * tile]
        left_hot = (cols[:, 0:1] == lane_rows).astype(bf16)
        rel_hot = (cols[:, 2:3] == lane_rel).astype(bf16)
        right_hot = cols[:, 1:2] == lane_rows
        slot_at = y * block + t * tile + lax.broadcasted_iota(jnp.int32, (tile, 1), 0)
        active = (slot_at < cols[:, 3:4]).astype(f32)
        left_rows = dot(left_hot, left_tab[...])
        scaling = sum(dot(rel_hot, term) for term in rel_terms)
        queries = (left_rows * scaling).astype(bf16)
        scores = dot_nt(queries, far_tab[...])
        positive = jnp.sum(jnp.where(right_hot, scores, 0.0), axis=1, keepdims=True)
        masked = jnp.where(counts > 0.0, scores, -1e30)
        peak = jnp.maximum(positive, jnp.max(masked, axis=1, keepdims=True))
        shifted = jnp.exp(masked - peak)
        pos_exp = jnp.exp(positive - peak)
        denom = pos_exp + jnp.sum(counts * shifted, axis=1, keepdims=True)
        weights = (shifted * (active / denom)).astype(bf16).astype(f32)
        pos_coef = active * (pos_exp / denom - 1.0)
        coef = counts * weights + jnp.where(right_hot, pos_coef, 0.0)
        high, low = parts_of(coef, 2)
        query_grad = dot(high, far_tab[...]) + dot(low, far_tab[...])
        far_part = dot_tn(high, queries) + dot_tn(low, queries)
        g_high, g_low = parts_of(query_grad * scaling, 2)
        own_part = dot_tn(left_hot, g_high) + dot_tn(left_hot, g_low)
        r_high, r_low = parts_of(query_grad * left_rows, 2)
        rel_part = dot_tn(rel_hot, r_high) + dot_tn(rel_hot, r_low)
        if t == 0:
            far_grad[...] = far_part
            own_grad[...] = own_part
            rg_out[...] = rel_part
        else:
            far_grad[...] += far_part
            own_grad[...] += own_part
            rg_out[...] += rel_part

    fgb[...] = far_grad[...].astype(bf16)
    c_far = copy(7, fgb, from_mate, mate)
    c_far.start()
    c_far.wait()
    both[...] = (own_grad[...] + from_mate[...].astype(f32)).astype(bf16)

    c_home = copy(8, both, from_y, ypeer)
    c_away = copy(8, both.at[other], from_y.at[other], ypeer)
    c_away_in = copy(8, both.at[mine], from_y.at[mine], ypeer)
    c_fin = copy(9, fin_send, fin.at[mine], diag)
    c_fin_y = copy(10, fin.at[mine], fin.at[mine], ypeer)
    c_fin_y_in = copy(10, fin.at[other], fin.at[other], ypeer)

    def finish(grad):
        state = state_in[...].T[:, 0:1]
        updated = state + jnp.sum(grad * grad, axis=1, keepdims=True) * (1.0 / width)
        ent_out[...] = ent[...] - entity_rate * grad / jnp.sqrt(updated)
        state_out[...] = jnp.broadcast_to(updated, (rows, 128)).T[:8]

    @pl.when(home)
    def _():
        c_home.start()
        c_home.wait()
        finish(both[...].astype(f32) + from_y[...].astype(f32))
        c_left.wait_send()
        c_cross.wait_send()
        c_mate0.wait_send()
        c_mate1.wait_send()

    @pl.when(away)
    def _():
        c_away.start()
        c_away_in.wait_recv()
        fin_send[...] = (both[mine, :].astype(f32) + from_y[mine, :].astype(f32)).astype(bf16)
        c_fin.start()
        c_fin.wait_recv()
        c_fin_y.start()
        c_fin_y_in.wait_recv()
        finish(fin[...].astype(f32))
        c_stage.wait_send()
        c_away.wait_send()
        c_fin.wait_send()
        c_fin_y.wait_send()


def local(
    entities, entity_state, relations, relation_state, edge_ends, relation_ids, neg_ids, edge_count
):
    rows, width = entities.shape
    nrel = relations.shape[0]
    slots = edge_ends.shape[1]
    blocks = neg_ids.shape[0]
    block = slots // blocks
    info = jnp.concatenate(
        [
            edge_ends,
            relation_ids[None],
            jnp.broadcast_to(edge_count[:, None], (1, slots)),
            neg_ids.reshape(1, -1),
            jnp.zeros((3, slots), jnp.int32),
        ],
        axis=0,
    )
    state8 = jnp.broadcast_to(entity_state[None], (8, rows))
    vmem = pl.BlockSpec(memory_space=pltpu.VMEM)
    table = pltpu.VMEM((rows, width), bf16)
    half_table = pltpu.VMEM((rows // 2, width), bf16)
    total = pltpu.VMEM((rows, width), f32)
    new_entities, state_rows, rel_grad = pl.pallas_call(
        functools.partial(kernel, lax.axis_size("dom"), block, min(256, block)),
        out_shape=(
            jax.ShapeDtypeStruct((rows, width), f32),
            jax.ShapeDtypeStruct((8, rows), f32),
            jax.ShapeDtypeStruct((nrel, width), f32),
        ),
        in_specs=[vmem] * 4,
        out_specs=(vmem,) * 3,
        scratch_shapes=[
            table,
            table,
            half_table,
            pltpu.VMEM((2, 8, slots), jnp.int32),
            total,
            total,
            table,
            table,
            table,
            table,
            half_table,
            table,
            pltpu.SemaphoreType.DMA((12,)),
            pltpu.SemaphoreType.DMA((12,)),
        ],
        compiler_params=pltpu.CompilerParams(
            collective_id=0, has_side_effects=True, vmem_limit_bytes=56 * 1024 * 1024
        ),
    )(entities, info, state8, relations)
    rel_total = lax.psum(rel_grad, ("dom", "bucket", "depth"))
    rel_state = relation_state + jnp.mean(rel_total * rel_total, axis=1)
    new_relations = relations - relation_rate * rel_total / jnp.sqrt(rel_state)[:, None]
    return (new_entities, state_rows[0], new_relations)


def solution(mesh):
    return jax.shard_map(
        local,
        mesh=mesh,
        in_specs=(
            P(("dom", "bucket"), None),
            P(("dom", "bucket")),
            P(),
            P(),
            P(None, ("dom", "bucket")),
            P(("dom", "bucket")),
            P(("dom", "bucket"), "depth"),
            P(("dom", "bucket")),
        ),
        out_specs=(P(("dom", "bucket"), None), P(("dom", "bucket")), P()),
        check_vma=False,
    )
```

time: 366 us -> 224 us (0.61)
  waiting for transfers between devices: 203 us -> 128 us
  Pallas kernels: 0 us -> 63.9 us
  other arithmetic: 60.8 us -> 2.33 us
  local copies, waits for them, and re-layouts: 39 us -> 11.9 us
  matrix products: 22.5 us -> 0 us
  blocking collectives: 21.7 us -> 0 us
    pallas_call x0 -> x1, Pallas kernels: none -> 63.9 us  [local(): pl.pallas_call(functools.partial(kernel, lax.axis_size('dom'), block, min...]
    reduce_scatter x2 -> x0, waiting for transfers between devices: 53.5 us -> none  [the longest x1 28.4 us: local(): lax.psum_scatter(own_grad, 'depth', scatter_dimension=0, tiled=True)]
    ppermute x2 -> x0, waiting for transfers between devices: 47.4 us -> none  [passed_along(): return lax.ppermute(block, axis, route)]
    scatter-add x8 -> x0, other arithmetic: 43.3 us -> none  [the longest x4 20.1 us: grad_part(): far_grad = far_grad.at[right_ids].add(half_coef[:, None] * queries.astype...]
    psum x1, waiting for transfers between devices: 102 us -> 128 us  [local(): rel_total = lax.psum(rel_grad, ('dom', 'bucket', 'depth'))]
    dot_general x12 -> x0, matrix products: 22.5 us -> none  [the longest x6 12.7 us: pick_rows(): jnp.dot(selector, table, preferred_element_type=jnp.float32)]
    all_gather x5 -> x0, blocking collectives: 21.7 us -> none  [the longest x4 17.3 us: merged(): pieces = jax.tree.map(lambda part: lax.all_gather(part, axis), value)]
    mul x6 -> x0, local copies, waits for them, and re-layouts: 14.7 us -> none  [the longest x2 4.93 us: grad_part(): query_grad * left_rows.astype(jnp.float32)]
  transfers between devices with their start and end apart: 6 -> 1, of which waited for: 5 -> 1; matrix products, arithmetic and copies ran while one was open for 3% -> 2% of each run, Pallas kernels for 0% -> 0%
where the time goes in v1:
time: 224 us; the launch traced here: 221 us
  waiting for transfers between devices  128 us (57%)
  Pallas kernels  63.9 us (29%)
  between operations  14.7 us (7%)
  local copies, waits for them, and re-layouts  11.9 us (5%)
  other arithmetic  2.33 us (1%)
    psum x1, waiting for transfers between devices, local(): rel_total = lax.psum(rel_grad, ('dom', 'bucket', 'depth'))  128 us
    pallas_call x1, Pallas kernels, local(): pl.pallas_call(functools.partial(kernel, lax.axis_size('dom'), block, min...  63.9 us
    unnamed x15, local copies, waits for them, and re-layouts  9.3 us
  transfers between devices with their start and end apart: 1, of which 1 were waited for; matrix products, arithmetic and copies ran while one was open for 2% of the time, Pallas kernels for 0%

profile of v1, /device:TPU:24, one launch (start us, length us, event | category | flops | bytes accessed | tf_op | source)
XLA Modules:
  0.0 220.7 jit_solution(4735511049009259190)
XLA Ops:
  7.2 0.0 all-reduce.2.cloned.1.call-start
  7.9 0.7 copy.16
  8.5 2.0 copy.12.rel
  10.6 0.0 copy-start.1
  10.6 0.0 copy-start.2
  10.6 0.0 copy-start.3
  10.6 2.9 %copy.11.ent = f32[1024,400]{1,0:T(8,128)} copy(f32[1024,400]{0,1:T(8,128)} %param.8) | data formatting | bytes 3276800 | tf_op args[0]
  13.4 0.0 copy-done.1
  13.4 0.0 copy-done.2
  13.4 0.7 concatenate.3.info_in
  14.1 0.0 copy-done.3
  14.1 0.6 broadcast_in_dim.25.state_in
  14.7 63.9 %shard_map.103 = (f32[1024,400]{1,0:T(8,128)}, f32[8,1024]{1,0:T(8,128)}, f32[256,400]{1,0:T(8,128)}) custom-call(f32[1024,400]{1,0:T(8,128)} %copy.11.ent, s32[8,1024]{1,0:T(8,128)} %concatenate.3.info_in, f32[8,1024]{1,0:T(8,128)} %broadcast_in_dim.25.state_in, f32[256,400]{1,0:T(8,128)} %copy.12.rel), custom_call_target="tpu_custom_call" | custom-call | tf_op jit(solution)/shard_map/pallas_call | solution.py:250
  78.6 0.0 all-reduce.2.cloned.1.call-update
  78.6 0.0 copy-start.4
  78.6 0.0 copy-start
  78.6 2.8 %copy.14 = f32[1024,400]{0,1:T(8,128)} copy(f32[1024,400]{1,0:T(8,128)} %get-tuple-element.9) | data formatting | bytes 3276800
  81.4 1.4 slice.3
  82.8 127.8 %all-reduce.2.cloned.1.call-done = f32[256,400]{1,0:T(8,128)} async-done(((f32[256,400]{1,0:T(8,128)}), f32[256,400]{1,0:T(8,128)}) %all-reduce.2.cloned.1.call-update) | async-done | bytes 409616 | tf_op jit(solution)/shard_map/psum | solution.py:279
  210.6 1.2 multiply_reduce_fusion
  211.8 0.0 copy-done.4
  211.8 0.0 copy-done
  211.8 1.2 divide_subtract_fusion
  213.0 0.9 copy.15
  (3 shorter events, 0.0 us)
Async XLA Ops:
  7.2 203.4 %all-reduce.2.cloned.1.call-start = ((), (), s32[]{:S(2)}) async-start(), calls=%async_computation | async-start | bytes 1048576 | tf_op jit(solution)/shard_map/psum | solution.py:279
  10.6 2.9 %copy-start.1 = (s32[2,1024]{1,0:T(2,128)S(1)}, s32[2,1024]{1,0:T(2,128)}, u32[]{:S(2)}) copy-start(s32[2,1024]{1,0:T(2,128)} %param.12) | copy-start | bytes 24580
  10.6 2.9 %copy-start.2 = (s32[1024]{0:T(1024)S(1)}, s32[1024]{0:T(1024)}, u32[]{:S(2)}) copy-start(s32[1024]{0:T(1024)} %param.13) | copy-start | bytes 12292
  10.6 3.5 %copy-start.3 = (f32[1024]{0:T(1024)S(1)}, f32[1024]{0:T(1024)}, u32[]{:S(2)}) copy-start(f32[1024]{0:T(1024)} %param.9) | copy-start | bytes 12292
  78.6 133.2 %copy-start.4 = (f32[256]{0:T(256)S(1)}, f32[256]{0:T(256)}, u32[]{:S(2)}) copy-start(f32[256]{0:T(256)} %param.11) | copy-start | bytes 3076
  78.6 133.2 %copy-start = (f32[256,400]{1,0:T(8,128)S(1)}, f32[256,400]{1,0:T(8,128)}, u32[]{:S(2)}) copy-start(f32[256,400]{1,0:T(8,128)} %copy.12.rel) | copy-start | bytes 1228804
Sparse Core Ops, SparseCore 0:
  78.7 131.8 all-reduce.1

commit v2 on v1

v2 whole, which is shorter than its diff:
```python
import functools

import jax
import jax.numpy as jnp
from jax import lax
from jax.experimental import pallas as pl
from jax.experimental.pallas import tpu as pltpu
from jax.sharding import PartitionSpec as P

entity_rate = 0.1
relation_rate = 1.0
MESH = pl.DeviceIdType.MESH
f32, bf16 = jnp.float32, jnp.bfloat16


def dot(a, b):
    return jnp.dot(a, b, preferred_element_type=f32)


def dot_nt(a, b):
    return lax.dot_general(a, b, (((1,), (1,)), ((), ())), preferred_element_type=f32)


def parts_of(value, terms):
    out = []
    for _ in range(terms):
        out.append(value.astype(bf16))
        value = value - out[-1].astype(f32)
    return out


def kernel(
    n_dom,
    block,
    neg_half,
    chunks,
    update_relations,
    ent,
    info_in,
    state_in,
    rel,
    rel_state,
    ent_out,
    state_out,
    rel_out,
    left_tab,
    far_tab,
    stage,
    info,
    own_grad,
    fgb,
    from_mate,
    both,
    from_y,
    fin_send,
    fin,
    rg,
    rs0,
    r1,
    rs1,
    r2,
    rs2,
    tot,
    ssem,
    rsem,
):
    width, rows = ent.shape
    nrel = rel.shape[1]
    half_rows = rows // 2
    chunk = half_rows // chunks
    d, b, y = lax.axis_index("dom"), lax.axis_index("bucket"), lax.axis_index("depth")
    half = n_dom // 2
    d2 = lax.rem(d + half, n_dom)
    odd = lax.rem(b, 2)
    b2 = b + 1 - 2 * odd
    y2 = 1 - y
    home = odd == d // half
    away = odd != d // half
    partner, mate, ypeer = (d2, b, y), (d, b2, y), (d, b, y2)
    diag, diag2 = (d2, b2, y), (d2, b2, y2)
    used = [0]

    def lanes(side, j=None):
        if j is None:
            return pl.ds(pl.multiple_of(side * half_rows, half_rows), half_rows)
        return pl.ds(pl.multiple_of(side * half_rows + j * chunk, chunk), chunk)

    def slots(count):
        used[0] += count
        return used[0] - count

    def copy(k, src, dst, device):
        return pltpu.make_async_remote_copy(
            src_ref=src,
            dst_ref=dst,
            send_sem=ssem.at[k],
            recv_sem=rsem.at[k],
            device_id=device,
            device_id_type=MESH,
        )

    def move(k, src, dst, side, device):
        return [
            copy(k + j, src.at[:, lanes(side, j)], dst.at[:, lanes(side, j)], device)
            for j in range(chunks)
        ]

    ring = [lax.rem(d + k, n_dom) for k in range(n_dom)]
    barrier = pltpu.get_barrier_semaphore()
    greeted = [mate, ypeer, diag, diag2] + [(ring[k], b, y) for k in range(1, n_dom)]
    for device in greeted:
        pl.semaphore_signal(barrier, inc=1, device_id=device, device_id_type=MESH)
    pl.semaphore_wait(barrier, len(greeted))

    c_info_home = copy(slots(1), info_in, info.at[1], ypeer)
    c_info_away2 = copy(used[0] - 1, info_in, info.at[1], diag2)
    c_info_away = copy(slots(1), info_in, info.at[0], diag)
    c_left = copy(slots(1), left_tab, far_tab, mate)
    c_stage = move(slots(chunks), stage, far_tab, y, partner)
    k_cross = slots(chunks)
    c_cross = move(k_cross, far_tab, far_tab, y, ypeer)
    c_cross_in = move(k_cross, far_tab, far_tab, y2, ypeer)
    c_mate0 = move(slots(chunks), far_tab, left_tab, y, mate)
    c_mate1 = move(slots(chunks), far_tab, left_tab, y2, mate)

    @pl.when(away)
    def _():
        for j in range(chunks):
            stage[:, lanes(y, j)] = ent[:, lanes(y, j)].astype(bf16)
            c_stage[j].start()
        c_info_away.start()
        c_info_away2.start()
        c_info_away.wait()
        c_info_away2.wait()

    @pl.when(home)
    def _():
        left_tab[...] = ent[...].astype(bf16)
        c_left.start()
        c_info_home.start()
        info[0] = info_in[...]
        c_info_home.wait()

    row_at = lax.broadcasted_iota(jnp.int32, (rows, 1), 0)
    rel_at = lax.broadcasted_iota(jnp.int32, (nrel, 1), 0)
    neg_lanes = pl.ds(pl.multiple_of(y * neg_half, neg_half), neg_half)
    edge_lanes = pl.ds(pl.multiple_of(y * block, block), block)
    counts = jnp.zeros((rows, 1), f32)
    for slot in range(2):
        ids = info[slot, 4:5, neg_lanes]
        counts += jnp.sum((row_at == ids).astype(f32), axis=1, keepdims=True)
    left_ids = info[0, 0:1, edge_lanes]
    right_ids = info[0, 1:2, edge_lanes]
    rel_ids = info[0, 2:3, edge_lanes]
    live = info[0, 3:4, edge_lanes]
    slot_at = y * block + lax.broadcasted_iota(jnp.int32, (1, block), 1)
    active = (slot_at < live).astype(f32)
    left_hot = (row_at == left_ids).astype(bf16)
    rel_hot = (rel_at == rel_ids).astype(bf16)
    scales = dot(jnp.concatenate(parts_of(rel[...], 3), axis=0), rel_hot)
    scaling = scales[:width] + scales[width : 2 * width] + scales[2 * width :]

    @pl.when(home)
    def _():
        for j in range(chunks):
            c_stage[j].wait_recv()
            c_cross[j].start()
            c_mate0[j].start()
        for j in range(chunks):
            c_cross_in[j].wait_recv()
            c_mate1[j].start()

    @pl.when(away)
    def _():
        c_left.wait_recv()
        for j in range(chunks):
            c_mate0[j].wait_recv()
        for j in range(chunks):
            c_mate1[j].wait_recv()

    left_rows = dot(left_tab[...], left_hot)
    queries = (left_rows * scaling).astype(bf16)
    far = far_tab[...]
    scores = dot(far.T, queries)
    right_hot = row_at == right_ids
    positive = jnp.sum(jnp.where(right_hot, scores, 0.0), axis=0, keepdims=True)
    masked = jnp.where(counts > 0.0, scores, -1e30)
    peak = jnp.maximum(positive, jnp.max(masked, axis=0, keepdims=True))
    shifted = jnp.exp(masked - peak)
    pos_exp = jnp.exp(positive - peak)
    denom = pos_exp + jnp.sum(counts * shifted, axis=0, keepdims=True)
    weights = (shifted * (active / denom)).astype(bf16).astype(f32)
    pos_coef = active * (pos_exp / denom - 1.0)
    high, low = parts_of(counts * weights + jnp.where(right_hot, pos_coef, 0.0), 2)
    query_grad = dot(far, high) + dot(far, low)

    rel_part = dot_nt(jnp.concatenate(parts_of(query_grad * left_rows, 2), axis=0), rel_hot)
    rel_part = rel_part[:width] + rel_part[width:]
    deep = rg.shape[1]
    for side in range(2):
        rg[side, :width] = rel_part[:, side * (nrel // 2) : (side + 1) * (nrel // 2)]
        rg[side, width:] = jnp.zeros((deep - width, nrel // 2), f32)
    odd2 = 1 - odd
    c_r0 = copy(slots(1), rg.at[odd2], rs0, mate)
    c_r0.start()

    fgb[...] = (dot_nt(queries, high) + dot_nt(queries, low)).astype(bf16)
    k_far = slots(2)
    c_far = [
        copy(k_far + i, fgb.at[:, lanes(s)], from_mate.at[:, lanes(s)], mate)
        for i, s in enumerate((y2, y))
    ]
    c_far[0].start()
    c_far[1].start()

    c_r0.wait_recv()
    r1[...] = rg[odd] + rs0[...]
    half_deep = deep // 2
    part = half_deep // n_dom
    mine_deep = pl.ds(pl.multiple_of(y * half_deep, half_deep), half_deep)
    other_deep = pl.ds(pl.multiple_of(y2 * half_deep, half_deep), half_deep)
    c_r1 = copy(slots(1), r1.at[other_deep], rs1, ypeer)
    c_r1.start()

    own_grad[...] = dot_nt((query_grad * scaling).astype(bf16), left_hot)
    k_away = slots(chunks)
    c_away = move(k_away, both, from_y, y2, ypeer)
    c_away_in = move(k_away, both, from_y, y, ypeer)
    k_home = slots(2)
    c_home = [
        copy(k_home + i, both.at[:, lanes(s)], from_y.at[:, lanes(s)], ypeer)
        for i, s in enumerate((y2, y))
    ]
    c_home_in = [
        copy(k_home + i, both.at[:, lanes(s)], from_y.at[:, lanes(s)], ypeer)
        for i, s in enumerate((y, y2))
    ]
    c_fin = move(slots(chunks), fin_send, fin, y, diag)
    k_fin_y = slots(chunks)
    c_fin_y = move(k_fin_y, fin, fin, y, ypeer)
    c_fin_y_in = move(k_fin_y, fin, fin, y2, ypeer)

    for i, s in enumerate((y2, y)):
        c_far[i].wait_recv()
        side = lanes(s)
        both[:, side] = (own_grad[:, side] + from_mate[:, side].astype(f32)).astype(bf16)

        @pl.when(home)
        def _():
            c_home[i].start()

        if i == 0:

            @pl.when(away)
            def _():
                for c in c_away:
                    c.start()

    c_r1.wait_recv()
    r2[...] = r1[mine_deep, :] + rs1[...]

    def piece(at):
        return pl.ds(pl.multiple_of(at * part, part), part)

    def total_piece(at):
        return pl.ds(pl.multiple_of(y * half_deep + at * part, part), part)

    k_r2 = slots(n_dom)
    c_r2 = [
        copy(k_r2 + k, r2.at[piece(ring[k])], rs2.at[k], (ring[k], b, y)) for k in range(1, n_dom)
    ]
    for c in c_r2:
        c.start()

    @pl.when(away)
    def _():
        for j in range(chunks):
            c_away_in[j].wait_recv()
            at = lanes(y, j)
            fin_send[:, at] = (both[:, at].astype(f32) + from_y[:, at].astype(f32)).astype(bf16)
            c_fin[j].start()

    for c in c_r2:
        c.wait_recv()
    tot[odd, total_piece(d), :] = r2[piece(d), :] + jnp.sum(rs2[1:], axis=0)
    k_t2 = slots(n_dom)
    here = tot.at[odd, total_piece(d)]
    c_t2 = [copy(k_t2 + k, here, here, (ring[k], b, y)) for k in range(1, n_dom)]
    c_t2_in = []
    for k in range(1, n_dom):
        there = tot.at[odd, total_piece(ring[n_dom - k])]
        c_t2_in.append(copy(k_t2 + k, there, there, (ring[k], b, y)))
    for c in c_t2:
        c.start()

    def finish(at, grad):
        updated = state_in[:, at] + jnp.sum(grad * grad, axis=0, keepdims=True) * (1.0 / width)
        ent_out[:, at] = ent[:, at] - grad * (entity_rate / jnp.sqrt(updated))
        state_out[:, at] = updated

    @pl.when(home)
    def _():
        for i, s in enumerate((y, y2)):
            c_home_in[i].wait_recv()
            at = lanes(s)
            finish(at, both[:, at].astype(f32) + from_y[:, at].astype(f32))

    @pl.when(away)
    def _():
        for j in range(chunks):
            c_fin[j].wait_recv()
            c_fin_y[j].start()

    for c in c_t2_in:
        c.wait_recv()
    mine_t, other_t = tot.at[odd, mine_deep], tot.at[odd, other_deep]
    k_t1 = slots(1)
    c_t1 = copy(k_t1, mine_t, mine_t, ypeer)
    c_t1_in = copy(k_t1, other_t, other_t, ypeer)
    c_t1.start()

    @pl.when(away)
    def _():
        for j in range(chunks):
            finish(lanes(y, j), fin[:, lanes(y, j)].astype(f32))

    c_t1_in.wait_recv()
    k_t0 = slots(1)
    c_t0 = copy(k_t0, tot.at[odd], tot.at[odd], mate)
    c_t0_in = copy(k_t0, tot.at[odd2], tot.at[odd2], mate)
    c_t0.start()

    @pl.when(away)
    def _():
        for j in range(chunks):
            c_fin_y_in[j].wait_recv()
            finish(lanes(y2, j), fin[:, lanes(y2, j)].astype(f32))

    c_t0_in.wait_recv()
    for side in range(2):
        at = pl.ds(side * (nrel // 2), nrel // 2)
        grad = tot[side, :width]
        if update_relations:
            updated = rel_state[:, at] + jnp.sum(grad * grad, axis=0, keepdims=True) * (1.0 / width)
            rel_out[:, at] = rel[:, at] - grad * (relation_rate / jnp.sqrt(updated))
        else:
            rel_out[:, at] = grad

    @pl.when(home)
    def _():
        for c in [c_left] + c_cross + c_mate0 + c_mate1 + c_home:
            c.wait_send()

    @pl.when(away)
    def _():
        for c in c_stage + c_away + c_fin + c_fin_y:
            c.wait_send()

    for c in [c_r0, c_r1, c_t1, c_t0] + c_far + c_r2 + c_t2:
        c.wait_send()


def local(
    entities, entity_state, relations, relation_state, edge_ends, relation_ids, neg_ids, edge_count
):
    rows, width = entities.shape
    nrel = relations.shape[0]
    slots = edge_ends.shape[1]
    blocks, neg_half = neg_ids.shape
    n_dom, n_bucket, n_depth = (lax.axis_size(a) for a in ("dom", "bucket", "depth"))
    assert blocks == n_depth == 2 and n_dom % 2 == 0 and n_bucket % 2 == 0
    assert blocks * neg_half == slots
    update_relations = n_bucket == 2
    chunks = max(1, rows // 2 // 128)
    info = jnp.concatenate(
        [
            edge_ends,
            relation_ids[None],
            jnp.broadcast_to(edge_count[:, None], (1, slots)),
            neg_ids.reshape(1, -1),
            jnp.zeros((3, slots), jnp.int32),
        ],
        axis=0,
    )
    grain = 2 * 8 * n_dom
    deep = -(-width // grain) * grain
    vmem = pl.BlockSpec(memory_space=pltpu.VMEM)
    table = pltpu.VMEM((width, rows), bf16)
    half_rel = nrel // 2
    n_sems = 5 + 7 * chunks + 2 + 2 + 2 * n_dom + 4
    new_ent, new_state, new_rel = pl.pallas_call(
        functools.partial(kernel, n_dom, slots // blocks, neg_half, chunks, update_relations),
        out_shape=(
            jax.ShapeDtypeStruct((width, rows), f32),
            jax.ShapeDtypeStruct((1, rows), f32),
            jax.ShapeDtypeStruct((width, nrel), f32),
        ),
        in_specs=[vmem] * 5,
        out_specs=(vmem,) * 3,
        scratch_shapes=[
            table,
            table,
            table,
            pltpu.VMEM((2, 8, slots), jnp.int32),
            pltpu.VMEM((width, rows), f32),
            table,
            table,
            table,
            table,
            table,
            table,
            pltpu.VMEM((2, deep, half_rel), f32),
            pltpu.VMEM((deep, half_rel), f32),
            pltpu.VMEM((deep, half_rel), f32),
            pltpu.VMEM((deep // 2, half_rel), f32),
            pltpu.VMEM((deep // 2, half_rel), f32),
            pltpu.VMEM((n_dom, deep // 2 // n_dom, half_rel), f32),
            pltpu.VMEM((2, deep, half_rel), f32),
            pltpu.SemaphoreType.DMA((n_sems,)),
            pltpu.SemaphoreType.DMA((n_sems,)),
        ],
        compiler_params=pltpu.CompilerParams(
            collective_id=0, has_side_effects=True, vmem_limit_bytes=56 * 1024 * 1024
        ),
    )(entities.T, info, entity_state[None], relations.T, relation_state[None])
    if not update_relations:
        total = 0.5 * lax.psum(new_rel, "bucket")
        updated = relation_state + jnp.mean(total * total, axis=0)
        new_rel = relations.T - relation_rate * total / jnp.sqrt(updated)[None]
    return (new_ent.T, new_state[0], new_rel.T)


def solution(mesh):
    return jax.shard_map(
        local,
        mesh=mesh,
        in_specs=(
            P(("dom", "bucket"), None),
            P(("dom", "bucket")),
            P(),
            P(),
            P(None, ("dom", "bucket")),
            P(("dom", "bucket")),
            P(("dom", "bucket"), "depth"),
            P(("dom", "bucket")),
        ),
        out_specs=(P(("dom", "bucket"), None), P(("dom", "bucket")), P()),
        check_vma=False,
    )
```

time: 224 us -> 67.5 us (0.30)
  the two profiles are of different devices: /device:TPU:24 before, /device:TPU:1 now
where the time goes in v2:
time: 67.5 us; the launch traced here: 67.2 us
  Pallas kernels  59.7 us (88%)
  local copies, waits for them, and re-layouts  6.24 us (9%)
  between operations  1.31 us (2%)
    pallas_call x1, Pallas kernels, local(): pl.pallas_call(functools.partial(kernel, n_dom, slots // blocks, neg_half...  59.7 us
    unnamed x8, local copies, waits for them, and re-layouts  4.88 us

profile of v2, /device:TPU:1, one launch (start us, length us, event | category | flops | bytes accessed | tf_op | source)
XLA Modules:
  0.0 67.2 jit_solution(12755351730449727221)
XLA Ops:
  1.3 0.7 %copy.11 = s32[1,1,2,512]{3,1,2,0:T(1,128)S(1)} copy(s32[1,1,2,512]{3,2,1,0:T(2,128)} %bitcast.20) | data formatting | bytes 8192
  2.0 1.3 %concatenate.3.info_in = s32[8,1024]{1,0:T(8,128)} concatenate(s32[2,1024]{1,0:T(2,128)} %param.12, s32[1,1024]{1,0:T(1,128)} %bitcast.19, s32[1,1024]{1,0:T(1,128)S(1)} %broadcast_in_dim.22, s32[1,1024]{1,0:T(1,128)S(1)} %bitcast.17, s32[3,1024]{1,0:T(4,128)S(1)} %broadcast_in_dim.23), dimensions={0} | concatenate | bytes 65536 | tf_op jit(solution)/shard_map/concatenate | solution.py:375
  3.3 59.7 %shard_map.103 = (f32[400,1024]{1,0:T(8,128)}, f32[1,1024]{1,0:T(1,128)}, f32[400,256]{1,0:T(8,128)}) custom-call(f32[400,1024]{1,0:T(8,128)} %bitcast.14, s32[8,1024]{1,0:T(8,128)} %concatenate.3.info_in, f32[1,1024]{1,0:T(1,128)} %bitcast.18, f32[400,256]{1,0:T(8,128)} %bitcast.16, f32[1,256]{1,0:T(1,128)} %bitcast.22), custom_call_target="tpu_custom_call" | custom-call | tf_op jit(solution)/shard_map/pallas_call | solution.py:391
  63.0 0.0 copy-start.1
  63.0 0.0 copy-start
  63.1 2.8 %copy.16 = f32[1024,400]{0,1:T(8,128)} copy(f32[1024,400]{0,1:T(8,128)} %bitcast.13) | data formatting | bytes 3276800
  65.9 0.0 copy-done.1
  65.9 0.6 copy.17
  66.5 0.0 copy-done
  66.5 0.8 %copy.18 = f32[256,400]{0,1:T(8,128)} copy(f32[256,400]{0,1:T(8,128)S(1)} %bitcast.15) | data formatting | bytes 819200
  (2 shorter events, 0.0 us)
Async XLA Ops:
  63.0 2.9 %copy-start.1 = (f32[1,1024]{1,0:T(1,128)S(1)}, f32[1,1024]{1,0:T(1,128)}, u32[]{:S(2)}) copy-start(f32[1,1024]{1,0:T(1,128)} %get-tuple-element.7) | copy-start | bytes 12292
  63.0 3.4 %copy-start = (f32[400,256]{1,0:T(8,128)S(1)}, f32[400,256]{1,0:T(8,128)}, u32[]{:S(2)}) copy-start(f32[400,256]{1,0:T(8,128)} %get-tuple-element.8) | copy-start | bytes 1228804

commit v3 on v2

v3 whole, which is shorter than its diff:
```python
import functools

import jax
import jax.numpy as jnp
from jax import lax
from jax.experimental import pallas as pl
from jax.experimental.pallas import tpu as pltpu
from jax.sharding import PartitionSpec as P

entity_rate = 0.1
relation_rate = 1.0
MESH = pl.DeviceIdType.MESH
f32, bf16 = jnp.float32, jnp.bfloat16


def dot(a, b):
    return jnp.dot(a, b, preferred_element_type=f32)


def dot_nt(a, b):
    return lax.dot_general(a, b, (((1,), (1,)), ((), ())), preferred_element_type=f32)


def parts_of(value, terms):
    out = []
    for _ in range(terms):
        out.append(value.astype(bf16))
        value = value - out[-1].astype(f32)
    return out


def kernel(
    n_dom,
    block,
    neg_half,
    chunks,
    ent,
    ends_in,
    rel_ids_in,
    neg_in,
    count_in,
    rel,
    grad_out,
    rel_out,
    ent_v,
    info_in,
    left_tab,
    far_tab,
    stage,
    info,
    left_hot,
    high,
    low,
    fgb,
    from_mate,
    both,
    from_y,
    fin_send,
    fin,
    rg,
    rs0,
    r1,
    rs1,
    r2,
    rs2,
    r3,
    rs3,
    tot,
    ssem,
    rsem,
    lsem,
):
    width, rows = ent.shape
    nrel = rel.shape[1]
    half_rows = rows // 2
    chunk = half_rows // chunks
    d, b, y = lax.axis_index("dom"), lax.axis_index("bucket"), lax.axis_index("depth")
    half = n_dom // 2
    d2 = lax.rem(d + half, n_dom)
    odd = lax.rem(b, 2)
    b2 = b + 1 - 2 * odd
    y2 = 1 - y
    home = odd == d // half
    away = odd != d // half
    partner, mate, ypeer = (d2, b, y), (d, b2, y), (d, b, y2)
    diag, diag2 = (d2, b2, y), (d2, b2, y2)
    used = [0]

    def lanes(side, j=None):
        if j is None:
            return pl.ds(pl.multiple_of(side * half_rows, half_rows), half_rows)
        return pl.ds(pl.multiple_of(side * half_rows + j * chunk, chunk), chunk)

    def slots(count):
        used[0] += count
        return used[0] - count

    def copy(k, src, dst, device):
        return pltpu.make_async_remote_copy(
            src_ref=src,
            dst_ref=dst,
            send_sem=ssem.at[k],
            recv_sem=rsem.at[k],
            device_id=device,
            device_id_type=MESH,
        )

    def move(k, src, dst, side, device):
        return [
            copy(k + j, src.at[:, lanes(side, j)], dst.at[:, lanes(side, j)], device)
            for j in range(chunks)
        ]

    load_mine = pltpu.make_async_copy(ent.at[:, lanes(y)], ent_v.at[:, lanes(y)], lsem.at[0])
    load_other = pltpu.make_async_copy(ent.at[:, lanes(y2)], ent_v.at[:, lanes(y2)], lsem.at[1])
    load_mine.start()

    @pl.when(home)
    def _():
        load_other.start()

    info_in[0:2] = ends_in[...]
    info_in[2:3] = rel_ids_in[...]
    info_in[3:4] = jnp.broadcast_to(count_in[...], (1, info_in.shape[1]))
    for c in range(neg_in.shape[0]):
        info_in[4:5, c * neg_half : (c + 1) * neg_half] = neg_in[c : c + 1]
    info_in[5:] = jnp.zeros((info_in.shape[0] - 5, info_in.shape[1]), jnp.int32)

    x2 = d + 1 - 2 * lax.rem(d, 2)
    n_ring = n_dom // 2
    ring = [lax.rem(d + k, n_dom) for k in range(n_dom)]
    barrier = pltpu.get_barrier_semaphore()
    load_mine.wait()
    greeted = [mate, ypeer, diag, diag2] + [(ring[k], b, y) for k in range(1, n_dom)]
    for device in greeted:
        pl.semaphore_signal(barrier, inc=1, device_id=device, device_id_type=MESH)
    pl.semaphore_wait(barrier, len(greeted))

    c_info_home = copy(slots(1), info_in, info.at[1], ypeer)
    c_info_away2 = copy(used[0] - 1, info_in, info.at[1], diag2)
    c_info_away = copy(slots(1), info_in, info.at[0], diag)
    c_left = copy(slots(1), left_tab, far_tab, mate)
    c_stage = move(slots(chunks), stage, far_tab, y, partner)
    k_cross = slots(chunks)
    c_cross = move(k_cross, far_tab, far_tab, y, ypeer)
    c_cross_in = move(k_cross, far_tab, far_tab, y2, ypeer)
    c_mate0 = move(slots(chunks), far_tab, left_tab, y, mate)
    c_mate1 = move(slots(chunks), far_tab, left_tab, y2, mate)

    @pl.when(away)
    def _():
        for j in range(chunks):
            stage[:, lanes(y, j)] = ent_v[:, lanes(y, j)].astype(bf16)
            c_stage[j].start()
        c_info_away.start()
        c_info_away2.start()
        c_info_away.wait()
        c_info_away2.wait()

    @pl.when(home)
    def _():
        load_other.wait()
        left_tab[...] = ent_v[...].astype(bf16)
        c_left.start()
        c_info_home.start()
        info[0] = info_in[...]
        c_info_home.wait()

    row_at = lax.broadcasted_iota(jnp.int32, (rows, 1), 0)
    rel_at = lax.broadcasted_iota(jnp.int32, (nrel, 1), 0)
    neg_lanes = pl.ds(pl.multiple_of(y * neg_half, neg_half), neg_half)
    edge_lanes = pl.ds(pl.multiple_of(y * block, block), block)
    counts = jnp.zeros((rows, 1), f32)
    for slot in range(2):
        ids = info[slot, 4:5, neg_lanes]
        counts += jnp.sum((row_at == ids).astype(f32), axis=1, keepdims=True)
    left_ids = info[0, 0:1, edge_lanes]
    right_ids = info[0, 1:2, edge_lanes]
    rel_ids = info[0, 2:3, edge_lanes]
    live = info[0, 3:4, edge_lanes]
    slot_at = y * block + lax.broadcasted_iota(jnp.int32, (1, block), 1)
    active = (slot_at < live).astype(f32)
    left_hot[...] = (row_at == left_ids).astype(bf16)
    rel_hot = (rel_at == rel_ids).astype(bf16)
    scales = dot(jnp.concatenate(parts_of(rel[...], 3), axis=0), rel_hot)
    scaling = scales[:width] + scales[width : 2 * width] + scales[2 * width :]

    @pl.when(home)
    def _():
        for j in range(chunks):
            c_stage[j].wait_recv()
            c_cross[j].start()
            c_mate0[j].start()
        for j in range(chunks):
            c_cross_in[j].wait_recv()
            c_mate1[j].start()

    @pl.when(away)
    def _():
        c_left.wait_recv()
        for j in range(chunks):
            c_mate0[j].wait_recv()
        for j in range(chunks):
            c_mate1[j].wait_recv()

    left_rows = dot(left_tab[...], left_hot[...])
    queries = (left_rows * scaling).astype(bf16)
    far = far_tab[...]
    scores = dot(far.T, queries)
    right_hot = row_at == right_ids
    positive = jnp.sum(jnp.where(right_hot, scores, 0.0), axis=0, keepdims=True)
    masked = jnp.where(counts > 0.0, scores, -1e30)
    peak = jnp.maximum(positive, jnp.max(masked, axis=0, keepdims=True))
    shifted = jnp.exp(masked - peak)
    pos_exp = jnp.exp(positive - peak)
    denom = pos_exp + jnp.sum(counts * shifted, axis=0, keepdims=True)
    weights = (shifted * (active / denom)).astype(bf16).astype(f32)
    pos_coef = active * (pos_exp / denom - 1.0)
    high[...], low[...] = parts_of(counts * weights + jnp.where(right_hot, pos_coef, 0.0), 2)

    k_far = slots(2)
    c_far = []
    for i, s in enumerate((y2, y)):
        c_far.append(copy(k_far + i, fgb.at[:, lanes(s)], from_mate.at[:, lanes(s)], mate))
        far_part = dot_nt(queries, high[lanes(s), :]) + dot_nt(queries, low[lanes(s), :])
        fgb[:, lanes(s)] = far_part.astype(bf16)
        c_far[i].start()

    query_grad = dot(far, high[...]) + dot(far, low[...])
    own_terms = (query_grad * scaling).astype(bf16)

    k_away = slots(chunks)
    c_away = move(k_away, both, from_y, y2, ypeer)
    c_away_in = move(k_away, both, from_y, y, ypeer)
    k_home = slots(2)
    c_home, c_home_in = [], []
    for i, (s, o) in enumerate(((y2, y), (y, y2))):
        c_home.append(copy(k_home + i, both.at[:, lanes(s)], from_y.at[:, lanes(s)], ypeer))
        c_home_in.append(copy(k_home + i, both.at[:, lanes(o)], from_y.at[:, lanes(o)], ypeer))
    c_fin = move(slots(chunks), fin_send, fin, y, diag)
    k_fin_y = slots(chunks)
    c_fin_y = move(k_fin_y, fin, fin, y, ypeer)
    c_fin_y_in = move(k_fin_y, fin, fin, y2, ypeer)

    def own_half(i, s):
        own_part = dot_nt(own_terms, left_hot[lanes(s), :])
        c_far[i].wait_recv()
        both[:, lanes(s)] = (own_part + from_mate[:, lanes(s)].astype(f32)).astype(bf16)

        @pl.when(home)
        def _():
            c_home[i].start()

    own_half(0, y2)

    @pl.when(away)
    def _():
        for c in c_away:
            c.start()

    rel_part = dot_nt(jnp.concatenate(parts_of(query_grad * left_rows, 2), axis=0), rel_hot)
    rel_part = rel_part[:width] + rel_part[width:]
    deep = rg.shape[1]
    for side in range(2):
        rg[side, :width] = rel_part[:, side * (nrel // 2) : (side + 1) * (nrel // 2)]
        rg[side, width:] = jnp.zeros((deep - width, nrel // 2), f32)
    odd2 = 1 - odd
    c_r0 = copy(slots(1), rg.at[odd2], rs0, mate)
    c_r0.start()

    own_half(1, y)

    half_deep = deep // 2
    part = half_deep // n_ring
    x, xpeer, lap = lax.rem(d, 2), (x2, b, y), d // 2

    def half_piece(side):
        return pl.ds(pl.multiple_of(side * half_deep, half_deep), half_deep)

    def piece(side, at):
        return pl.ds(pl.multiple_of(side * half_deep + at * part, part), part)

    laps = [lax.rem(lap + k, n_ring) for k in range(n_ring)]
    peers = [(2 * at + x, b, y) for at in laps]

    c_r0.wait_recv()
    r1[...] = rg[odd] + rs0[...]
    c_r1 = copy(slots(1), r1.at[half_piece(1 - x)], rs1, xpeer)
    c_r1.start()
    c_r1.wait_recv()
    r2[...] = r1[half_piece(x), :] + rs1[...]
    k_r2 = slots(n_ring)
    c_r2 = [
        copy(k_r2 + k, r2.at[piece(0, laps[k])], rs2.at[k], peers[k]) for k in range(1, n_ring)
    ]
    for c in c_r2:
        c.start()

    @pl.when(away)
    def _():
        for j in range(chunks):
            c_away_in[j].wait_recv()
            at = lanes(y, j)
            fin_send[:, at] = (both[:, at].astype(f32) + from_y[:, at].astype(f32)).astype(bf16)
            c_fin[j].start()

    for c in c_r2:
        c.wait_recv()
    r3[...] = r2[piece(0, lap), :] + jnp.sum(rs2[1:], axis=0)
    c_r3 = copy(slots(1), r3, rs3, ypeer)
    c_r3.start()
    c_r3.wait_recv()
    tot[odd, piece(x, lap), :] = r3[...] + rs3[...]
    k_t2 = slots(n_ring)
    here = tot.at[odd, piece(x, lap)]
    c_t2, c_t2_in = [], []
    for k in range(1, n_ring):
        there = tot.at[odd, piece(x, laps[n_ring - k])]
        c_t2.append(copy(k_t2 + k, here, here, peers[k]))
        c_t2_in.append(copy(k_t2 + k, there, there, peers[k]))
        c_t2[-1].start()

    @pl.when(home)
    def _():
        c_home_in[0].wait_recv()
        at = lanes(y)
        grad_out[:, at] = both[:, at].astype(f32) + from_y[:, at].astype(f32)

    for c in c_t2_in:
        c.wait_recv()
    mine_t, other_t = tot.at[odd, half_piece(x)], tot.at[odd, half_piece(1 - x)]
    k_t1 = slots(1)
    c_t1 = copy(k_t1, mine_t, mine_t, xpeer)
    c_t1_in = copy(k_t1, other_t, other_t, xpeer)
    c_t1.start()

    @pl.when(away)
    def _():
        for j in range(chunks):
            c_fin[j].wait_recv()
            c_fin_y[j].start()

    c_t1_in.wait_recv()
    k_t0 = slots(1)
    c_t0 = copy(k_t0, tot.at[odd], tot.at[odd], mate)
    c_t0_in = copy(k_t0, tot.at[odd2], tot.at[odd2], mate)
    c_t0.start()

    @pl.when(away)
    def _():
        grad_out[:, lanes(y)] = fin[:, lanes(y)].astype(f32)
        for j in range(chunks):
            c_fin_y_in[j].wait_recv()
            grad_out[:, lanes(y2, j)] = fin[:, lanes(y2, j)].astype(f32)

    @pl.when(home)
    def _():
        c_home_in[1].wait_recv()
        at = lanes(y2)
        grad_out[:, at] = both[:, at].astype(f32) + from_y[:, at].astype(f32)

    c_t0_in.wait_recv()
    for side in range(2):
        rel_out[:, side * (nrel // 2) : (side + 1) * (nrel // 2)] = tot[side, :width]

    @pl.when(home)
    def _():
        for c in [c_left] + c_cross + c_mate0 + c_mate1 + c_home:
            c.wait_send()

    @pl.when(away)
    def _():
        for c in c_stage + c_away + c_fin + c_fin_y:
            c.wait_send()

    for c in [c_r0, c_r1, c_r3, c_t1, c_t0] + c_far + c_r2 + c_t2:
        c.wait_send()


def adagrad(rate, values, state, grad, values_out, state_out):
    updated = state[...] + jnp.sum(grad * grad, axis=0, keepdims=True) * (1.0 / grad.shape[0])
    values_out[...] = values[...] - grad * (rate / jnp.sqrt(updated))
    if state_out is not None:
        state_out[...] = updated


def update(ent, state, grad, rel, rel_state, rel_grad, ent_out, state_out, rel_out):
    adagrad(entity_rate, ent, state, grad[...], ent_out, state_out)

    @pl.when(pl.program_id(0) == 0)
    def _():
        adagrad(relation_rate, rel, rel_state, rel_grad[...], rel_out, None)


def local(
    entities, entity_state, relations, relation_state, edge_ends, relation_ids, neg_ids, edge_count
):
    rows, width = entities.shape
    nrel = relations.shape[0]
    slots = edge_ends.shape[1]
    blocks, neg_half = neg_ids.shape
    n_dom, n_bucket, n_depth = (lax.axis_size(a) for a in ("dom", "bucket", "depth"))
    assert blocks == n_depth == 2 and n_dom % 2 == 0 and n_bucket % 2 == 0
    assert blocks * neg_half == slots
    chunks = max(1, rows // 2 // 128)
    grain = 8 * n_dom
    deep = -(-width // grain) * grain
    half_rel = nrel // 2
    vmem = pl.BlockSpec(memory_space=pltpu.VMEM)
    table = pltpu.VMEM((width, rows), bf16)
    spots = pltpu.VMEM((rows, slots // blocks), bf16)
    n_sems = 16 + 7 * chunks + n_dom
    params = dict(vmem_limit_bytes=56 * 1024 * 1024)
    ent, rel = entities.T, relations.T
    grad, rel_grad = pl.pallas_call(
        functools.partial(kernel, n_dom, slots // blocks, neg_half, chunks),
        out_shape=(
            jax.ShapeDtypeStruct((width, rows), f32),
            jax.ShapeDtypeStruct((width, nrel), f32),
        ),
        in_specs=[pl.BlockSpec(memory_space=pl.ANY)] + [vmem] * 5,
        out_specs=(vmem,) * 2,
        scratch_shapes=[
            pltpu.VMEM((width, rows), f32),
            pltpu.VMEM((8, slots), jnp.int32),
            table,
            table,
            table,
            pltpu.VMEM((2, 8, slots), jnp.int32),
            spots,
            spots,
            spots,
            table,
            table,
            table,
            table,
            table,
            table,
            pltpu.VMEM((2, deep, half_rel), f32),
            pltpu.VMEM((deep, half_rel), f32),
            pltpu.VMEM((deep, half_rel), f32),
            pltpu.VMEM((deep // 2, half_rel), f32),
            pltpu.VMEM((deep // 2, half_rel), f32),
            pltpu.VMEM((n_dom // 2, deep // n_dom, half_rel), f32),
            pltpu.VMEM((deep // n_dom, half_rel), f32),
            pltpu.VMEM((deep // n_dom, half_rel), f32),
            pltpu.VMEM((2, deep, half_rel), f32),
            pltpu.SemaphoreType.DMA((n_sems,)),
            pltpu.SemaphoreType.DMA((n_sems,)),
            pltpu.SemaphoreType.DMA((2,)),
        ],
        compiler_params=pltpu.CompilerParams(collective_id=0, has_side_effects=True, **params),
    )(ent, edge_ends, relation_ids[None], neg_ids, edge_count[None], rel)
    if n_bucket != 2:
        rel_grad = 0.5 * lax.psum(rel_grad, "bucket")
    step = min(256, rows)
    wide = pl.BlockSpec((width, step), lambda i: (0, i))
    line = pl.BlockSpec((1, step), lambda i: (0, i))
    rel_all = pl.BlockSpec((width, nrel), lambda i: (0, 0))
    new_ent, new_state, new_rel = pl.pallas_call(
        update,
        grid=(rows // step,),
        out_shape=(
            jax.ShapeDtypeStruct((width, rows), f32),
            jax.ShapeDtypeStruct((1, rows), f32),
            jax.ShapeDtypeStruct((width, nrel), f32),
        ),
        in_specs=[wide, line, wide, rel_all, pl.BlockSpec((1, nrel), lambda i: (0, 0)), rel_all],
        out_specs=(wide, line, rel_all),
        compiler_params=pltpu.CompilerParams(**params),
    )(ent, entity_state[None], grad, rel, relation_state[None], rel_grad)
    return (new_ent.T, new_state[0], new_rel.T)


def solution(mesh):
    return jax.shard_map(
        local,
        mesh=mesh,
        in_specs=(
            P(("dom", "bucket"), None),
            P(("dom", "bucket")),
            P(),
            P(),
            P(None, ("dom", "bucket")),
            P(("dom", "bucket")),
            P(("dom", "bucket"), "depth"),
            P(("dom", "bucket")),
        ),
        out_specs=(P(("dom", "bucket"), None), P(("dom", "bucket")), P()),
        check_vma=False,
    )
```

time: 67.5 us -> 64 us (0.948)
  the two profiles are of different devices: /device:TPU:1 before, /device:TPU:24 now
where the time goes in v3:
time: 64 us; the launch traced here: 63.7 us
  Pallas kernels  62.4 us (98%)
  between operations  1.29 us (2%)
    pallas_call x1, Pallas kernels, local(): pl.pallas_call(functools.partial(kernel, n_dom, slots // blocks, neg_half...  57.8 us
    pallas_call x1, Pallas kernels, local(): pl.pallas_call(update, grid=(rows // step,), out_shape=(jax.ShapeDtypeStr...  4.66 us

profile of v3, /device:TPU:24, one launch (start us, length us, event | category | flops | bytes accessed | tf_op | source)
XLA Modules:
  0.0 63.7 jit_solution(14393590969003354262)
XLA Ops:
  1.3 57.8 %shard_map.103 = (f32[400,1024]{1,0:T(8,128)}, f32[400,256]{1,0:T(8,128)}) custom-call(f32[400,1024]{1,0:T(8,128)} %bitcast.10, s32[2,1024]{1,0:T(2,128)} %ends_in.1, s32[1,1024]{1,0:T(1,128)} %bitcast.14, s32[2,512]{1,0:T(2,128)} %neg_in.1, s32[1,1]{1,0:T(1,128)} %bitcast.9.count_in, f32[400,256]{1,0:T(8,128)} %bitcast.12), custom_call_target="tpu_custom_call" | custom-call | tf_op jit(solution)/shard_map/pallas_call | solution.py:415
  59.1 4.7 %shard_map.104 = (f32[400,1024]{1,0:T(8,128)}, f32[1,1024]{1,0:T(1,128)}, f32[400,256]{1,0:T(8,128)}) custom-call(f32[400,1024]{1,0:T(8,128)} %bitcast.11, f32[1,1024]{1,0:T(1,128)} %bitcast.15, f32[400,1024]{1,0:T(8,128)} %get-tuple-element.8.grad, f32[400,256]{1,0:T(8,128)} %bitcast.13, f32[1,256]{1,0:T(1,128)} %bitcast.16, ...), custom_call_target="tpu_custom_call" | custom-call | tf_op jit(solution)/shard_map/pallas_call | solution.py:460

commit v4 on v3

--- a/solution.py
+++ b/solution.py
@@ -10,6 +10,7 @@
 entity_rate = 0.1
 relation_rate = 1.0
 MESH = pl.DeviceIdType.MESH
+STRIP = 64
 f32, bf16 = jnp.float32, jnp.bfloat16
 
 
@@ -51,6 +52,8 @@
     left_hot,
     high,
     low,
+    scores,
+    counts,
     fgb,
     from_mate,
     both,
@@ -166,21 +169,37 @@
         info[0] = info_in[...]
         c_info_home.wait()
 
-    row_at = lax.broadcasted_iota(jnp.int32, (rows, 1), 0)
     rel_at = lax.broadcasted_iota(jnp.int32, (nrel, 1), 0)
     neg_lanes = pl.ds(pl.multiple_of(y * neg_half, neg_half), neg_half)
     edge_lanes = pl.ds(pl.multiple_of(y * block, block), block)
-    counts = jnp.zeros((rows, 1), f32)
-    for slot in range(2):
-        ids = info[slot, 4:5, neg_lanes]
-        counts += jnp.sum((row_at == ids).astype(f32), axis=1, keepdims=True)
     left_ids = info[0, 0:1, edge_lanes]
     right_ids = info[0, 1:2, edge_lanes]
     rel_ids = info[0, 2:3, edge_lanes]
     live = info[0, 3:4, edge_lanes]
     slot_at = y * block + lax.broadcasted_iota(jnp.int32, (1, block), 1)
     active = (slot_at < live).astype(f32)
-    left_hot[...] = (row_at == left_ids).astype(bf16)
+    negs = jnp.concatenate([info[slot, 4:5, neg_lanes] for slot in range(2)], axis=1)
+
+    def strip(i):
+        at = pl.ds(pl.multiple_of(i * STRIP, STRIP), STRIP)
+        return at, i * STRIP + lax.broadcasted_iota(jnp.int32, (STRIP, 1), 0)
+
+    def fold(value, join):
+        return join(value.reshape(STRIP // 8, 8, block), axis=0)
+
+    def spread(at):
+        return jnp.concatenate([counts[at, :]] * (block // 128), axis=1)
+
+    def find(i, carry):
+        at, row_at = strip(i)
+        hits = jnp.zeros((STRIP, 128), f32)
+        for t in range(2 * neg_half // 128):
+            hits += (row_at == negs[:, t * 128 : (t + 1) * 128]).astype(f32)
+        counts[at, :] = jnp.broadcast_to(jnp.sum(hits, axis=1, keepdims=True), (STRIP, 128))
+        left_hot[at, :] = (row_at == left_ids).astype(bf16)
+        return carry
+
+    lax.fori_loop(0, rows // STRIP, find, 0)
     rel_hot = (rel_at == rel_ids).astype(bf16)
     scales = dot(jnp.concatenate(parts_of(rel[...], 3), axis=0), rel_hot)
     scaling = scales[:width] + scales[width : 2 * width] + scales[2 * width :]
@@ -206,17 +225,43 @@
     left_rows = dot(left_tab[...], left_hot[...])
     queries = (left_rows * scaling).astype(bf16)
     far = far_tab[...]
-    scores = dot(far.T, queries)
-    right_hot = row_at == right_ids
-    positive = jnp.sum(jnp.where(right_hot, scores, 0.0), axis=0, keepdims=True)
-    masked = jnp.where(counts > 0.0, scores, -1e30)
-    peak = jnp.maximum(positive, jnp.max(masked, axis=0, keepdims=True))
-    shifted = jnp.exp(masked - peak)
+    scores[...] = dot(far.T, queries)
+
+    def largest(i, carry):
+        at, row_at = strip(i)
+        score = scores[at, :]
+        best = fold(jnp.where(spread(at) > 0.0, score, -1e30), jnp.max)
+        return (
+            jnp.maximum(carry[0], best),
+            carry[1] + fold(jnp.where(row_at == right_ids, score, 0.0), jnp.sum),
+        )
+
+    start = (jnp.full((8, block), -1e30, f32), jnp.zeros((8, block), f32))
+    best, hit = lax.fori_loop(0, rows // STRIP, largest, start)
+    positive = jnp.sum(hit, axis=0, keepdims=True)
+    peak = jnp.maximum(positive, jnp.max(best, axis=0, keepdims=True))
+
+    def exponentials(i, carry):
+        at, _ = strip(i)
+        count = spread(at)
+        shifted = jnp.exp(jnp.where(count > 0.0, scores[at, :], -1e30) - peak)
+        scores[at, :] = shifted
+        return carry + fold(count * shifted, jnp.sum)
+
+    total = lax.fori_loop(0, rows // STRIP, exponentials, jnp.zeros((8, block), f32))
     pos_exp = jnp.exp(positive - peak)
-    denom = pos_exp + jnp.sum(counts * shifted, axis=0, keepdims=True)
-    weights = (shifted * (active / denom)).astype(bf16).astype(f32)
+    denom = pos_exp + jnp.sum(total, axis=0, keepdims=True)
+    scale = active / denom
     pos_coef = active * (pos_exp / denom - 1.0)
-    high[...], low[...] = parts_of(counts * weights + jnp.where(right_hot, pos_coef, 0.0), 2)
+
+    def coefficients(i, carry):
+        at, row_at = strip(i)
+        weights = (scores[at, :] * scale).astype(bf16).astype(f32)
+        value = spread(at) * weights + jnp.where(row_at == right_ids, pos_coef, 0.0)
+        high[at, :], low[at, :] = parts_of(value, 2)
+        return carry
+
+    lax.fori_loop(0, rows // STRIP, coefficients, 0)
 
     k_far = slots(2)
     c_far = []
@@ -324,7 +369,7 @@
     def _():
         c_home_in[0].wait_recv()
         at = lanes(y)
-        grad_out[:, at] = both[:, at].astype(f32) + from_y[:, at].astype(f32)
+        grad_out[:, at] = (both[:, at].astype(f32) + from_y[:, at].astype(f32)).astype(bf16)
 
     for c in c_t2_in:
         c.wait_recv()
@@ -348,16 +393,16 @@
 
     @pl.when(away)
     def _():
-        grad_out[:, lanes(y)] = fin[:, lanes(y)].astype(f32)
+        grad_out[:, lanes(y)] = fin[:, lanes(y)]
         for j in range(chunks):
             c_fin_y_in[j].wait_recv()
-            grad_out[:, lanes(y2, j)] = fin[:, lanes(y2, j)].astype(f32)
+            grad_out[:, lanes(y2, j)] = fin[:, lanes(y2, j)]
 
     @pl.when(home)
     def _():
         c_home_in[1].wait_recv()
         at = lanes(y2)
-        grad_out[:, at] = both[:, at].astype(f32) + from_y[:, at].astype(f32)
+        grad_out[:, at] = (both[:, at].astype(f32) + from_y[:, at].astype(f32)).astype(bf16)
 
     c_t0_in.wait_recv()
     for side in range(2):
@@ -385,7 +430,7 @@
 
 
 def update(ent, state, grad, rel, rel_state, rel_grad, ent_out, state_out, rel_out):
-    adagrad(entity_rate, ent, state, grad[...], ent_out, state_out)
+    adagrad(entity_rate, ent, state, grad[...].astype(f32), ent_out, state_out)
 
     @pl.when(pl.program_id(0) == 0)
     def _():
@@ -415,7 +460,7 @@
     grad, rel_grad = pl.pallas_call(
         functools.partial(kernel, n_dom, slots // blocks, neg_half, chunks),
         out_shape=(
-            jax.ShapeDtypeStruct((width, rows), f32),
+            jax.ShapeDtypeStruct((width, rows), bf16),
             jax.ShapeDtypeStruct((width, nrel), f32),
         ),
         in_specs=[pl.BlockSpec(memory_space=pl.ANY)] + [vmem] * 5,
@@ -430,6 +475,8 @@
             spots,
             spots,
             spots,
+            pltpu.VMEM((rows, slots // blocks), f32),
+            pltpu.VMEM((rows, 128), f32),
             table,
             table,
             table,
@@ -453,7 +500,7 @@
     )(ent, edge_ends, relation_ids[None], neg_ids, edge_count[None], rel)
     if n_bucket != 2:
         rel_grad = 0.5 * lax.psum(rel_grad, "bucket")
-    step = min(256, rows)
+    step = max(128, rows // 2)
     wide = pl.BlockSpec((width, step), lambda i: (0, i))
     line = pl.BlockSpec((1, step), lambda i: (0, i))
     rel_all = pl.BlockSpec((width, nrel), lambda i: (0, 0))

time: 64 us -> 62 us (0.969)
  Pallas kernels: 62.4 us -> 60.6 us
    pallas_call x1, Pallas kernels: 4.66 us -> 3.2 us  [local(): pl.pallas_call(update, grid=(rows // step,), out_shape=(jax.ShapeDtypeStr...]
where the time goes in v4:
time: 62 us; the launch traced here: 61.8 us
  Pallas kernels  60.6 us (98%)
  between operations  1.29 us (2%)
    pallas_call x1, Pallas kernels, local(): pl.pallas_call(functools.partial(kernel, n_dom, slots // blocks, neg_half...  57.4 us
    pallas_call x1, Pallas kernels, local(): pl.pallas_call(update, grid=(rows // step,), out_shape=(jax.ShapeDtypeStr...  3.2 us

profile of v4, /device:TPU:24, one launch (start us, length us, event | category | flops | bytes accessed | tf_op | source)
XLA Modules:
  0.0 61.8 jit_solution(16988133326280396969)
XLA Ops:
  1.3 57.4 %shard_map.103 = (bf16[400,1024]{1,0:T(8,128)(2,1)}, f32[400,256]{1,0:T(8,128)}) custom-call(f32[400,1024]{1,0:T(8,128)} %bitcast.10, s32[2,1024]{1,0:T(2,128)} %ends_in.1, s32[1,1024]{1,0:T(1,128)} %bitcast.14, s32[2,512]{1,0:T(2,128)} %neg_in.1, s32[1,1]{1,0:T(1,128)} %bitcast.9.count_in, f32[400,256]{1,0:T(8,128)} %bitcast.12), custom_call_target="tpu_custom_call" | custom-call | tf_op jit(solution)/shard_map/pallas_call | solution.py:460
  58.6 3.2 %shard_map.104 = (f32[400,1024]{1,0:T(8,128)}, f32[1,1024]{1,0:T(1,128)}, f32[400,256]{1,0:T(8,128)}) custom-call(f32[400,1024]{1,0:T(8,128)} %bitcast.11, f32[1,1024]{1,0:T(1,128)} %bitcast.15, bf16[400,1024]{1,0:T(8,128)(2,1)} %get-tuple-element.8.grad, f32[400,256]{1,0:T(8,128)} %bitcast.13, f32[1,256]{1,0:T(1,128)} %bitcast.16, ...), custom_call_target="tpu_custom_call" | custom-call | tf_op jit(solution)/shard_map/pallas_call | solution.py:507

commit v5 on v4

--- a/solution.py
+++ b/solution.py
@@ -94,6 +94,18 @@
             return pl.ds(pl.multiple_of(side * half_rows, half_rows), half_rows)
         return pl.ds(pl.multiple_of(side * half_rows + j * chunk, chunk), chunk)
 
+    def spot(side, j):
+        return side * chunks + j
+
+    def group(side):
+        return pl.ds(side * chunks, chunks)
+
+    def whole(table):
+        return jnp.concatenate([table[j] for j in range(2 * chunks)], axis=1)
+
+    def cut(value, j):
+        return value[:, j * chunk : (j + 1) * chunk]
+
     def slots(count):
         used[0] += count
         return used[0] - count
@@ -110,7 +122,7 @@
 
     def move(k, src, dst, side, device):
         return [
-            copy(k + j, src.at[:, lanes(side, j)], dst.at[:, lanes(side, j)], device)
+            copy(k + j, src.at[spot(side, j)], dst.at[spot(side, j)], device)
             for j in range(chunks)
         ]
 
@@ -153,7 +165,7 @@
     @pl.when(away)
     def _():
         for j in range(chunks):
-            stage[:, lanes(y, j)] = ent_v[:, lanes(y, j)].astype(bf16)
+            stage[spot(y, j)] = ent_v[:, lanes(y, j)].astype(bf16)
             c_stage[j].start()
         c_info_away.start()
         c_info_away2.start()
@@ -163,7 +175,8 @@
     @pl.when(home)
     def _():
         load_other.wait()
-        left_tab[...] = ent_v[...].astype(bf16)
+        for j in range(2 * chunks):
+            left_tab[j] = cut(ent_v, j).astype(bf16)
         c_left.start()
         c_info_home.start()
         info[0] = info_in[...]
@@ -222,9 +235,9 @@
         for j in range(chunks):
             c_mate1[j].wait_recv()
 
-    left_rows = dot(left_tab[...], left_hot[...])
+    left_rows = dot(whole(left_tab), left_hot[...])
     queries = (left_rows * scaling).astype(bf16)
-    far = far_tab[...]
+    far = whole(far_tab)
     scores[...] = dot(far.T, queries)
 
     def largest(i, carry):
@@ -266,9 +279,10 @@
     k_far = slots(2)
     c_far = []
     for i, s in enumerate((y2, y)):
-        c_far.append(copy(k_far + i, fgb.at[:, lanes(s)], from_mate.at[:, lanes(s)], mate))
+        c_far.append(copy(k_far + i, fgb.at[group(s)], from_mate.at[group(s)], mate))
         far_part = dot_nt(queries, high[lanes(s), :]) + dot_nt(queries, low[lanes(s), :])
-        fgb[:, lanes(s)] = far_part.astype(bf16)
+        for j in range(chunks):
+            fgb[spot(s, j)] = cut(far_part, j).astype(bf16)
         c_far[i].start()
 
     query_grad = dot(far, high[...]) + dot(far, low[...])
@@ -280,8 +294,8 @@
     k_home = slots(2)
     c_home, c_home_in = [], []
     for i, (s, o) in enumerate(((y2, y), (y, y2))):
-        c_home.append(copy(k_home + i, both.at[:, lanes(s)], from_y.at[:, lanes(s)], ypeer))
-        c_home_in.append(copy(k_home + i, both.at[:, lanes(o)], from_y.at[:, lanes(o)], ypeer))
+        c_home.append(copy(k_home + i, both.at[group(s)], from_y.at[group(s)], ypeer))
+        c_home_in.append(copy(k_home + i, both.at[group(o)], from_y.at[group(o)], ypeer))
     c_fin = move(slots(chunks), fin_send, fin, y, diag)
     k_fin_y = slots(chunks)
     c_fin_y = move(k_fin_y, fin, fin, y, ypeer)
@@ -290,7 +304,9 @@
     def own_half(i, s):
         own_part = dot_nt(own_terms, left_hot[lanes(s), :])
         c_far[i].wait_recv()
-        both[:, lanes(s)] = (own_part + from_mate[:, lanes(s)].astype(f32)).astype(bf16)
+        for j in range(chunks):
+            at = spot(s, j)
+            both[at] = (cut(own_part, j) + from_mate[at].astype(f32)).astype(bf16)
 
         @pl.when(home)
         def _():
@@ -328,10 +344,40 @@
     laps = [lax.rem(lap + k, n_ring) for k in range(n_ring)]
     peers = [(2 * at + x, b, y) for at in laps]
 
+    def pass_on(j):
+        @pl.when(away)
+        def _():
+            at = spot(y, j)
+            c_away_in[j].wait_recv()
+            fin_send[at] = (both[at].astype(f32) + from_y[at].astype(f32)).astype(bf16)
+            c_fin[j].start()
+
+    def hand_over(j):
+        @pl.when(away)
+        def _():
+            c_fin[j].wait_recv()
+            c_fin_y[j].start()
+            grad_out[:, lanes(y, j)] = fin[spot(y, j)]
+
+    def take(i, side):
+        @pl.when(home)
+        def _():
+            c_home_in[i].wait_recv()
+            for j in range(chunks):
+                at = spot(side, j)
+                sums = both[at].astype(f32) + from_y[at].astype(f32)
+                grad_out[:, lanes(side, j)] = sums.astype(bf16)
+
+    steps = [[] for _ in range(5)]
+    for j in range(chunks):
+        steps[min(j, 4)].append(j)
+
     c_r0.wait_recv()
     r1[...] = rg[odd] + rs0[...]
     c_r1 = copy(slots(1), r1.at[half_piece(1 - x)], rs1, xpeer)
     c_r1.start()
+    for j in steps[0]:
+        pass_on(j)
     c_r1.wait_recv()
     r2[...] = r1[half_piece(x), :] + rs1[...]
     k_r2 = slots(n_ring)
@@ -340,20 +386,15 @@
     ]
     for c in c_r2:
         c.start()
-
-    @pl.when(away)
-    def _():
-        for j in range(chunks):
-            c_away_in[j].wait_recv()
-            at = lanes(y, j)
-            fin_send[:, at] = (both[:, at].astype(f32) + from_y[:, at].astype(f32)).astype(bf16)
-            c_fin[j].start()
-
+    for j in steps[1]:
+        pass_on(j)
     for c in c_r2:
         c.wait_recv()
     r3[...] = r2[piece(0, lap), :] + jnp.sum(rs2[1:], axis=0)
     c_r3 = copy(slots(1), r3, rs3, ypeer)
     c_r3.start()
+    for j in steps[2]:
+        pass_on(j)
     c_r3.wait_recv()
     tot[odd, piece(x, lap), :] = r3[...] + rs3[...]
     k_t2 = slots(n_ring)
@@ -364,13 +405,8 @@
         c_t2.append(copy(k_t2 + k, here, here, peers[k]))
         c_t2_in.append(copy(k_t2 + k, there, there, peers[k]))
         c_t2[-1].start()
-
-    @pl.when(home)
-    def _():
-        c_home_in[0].wait_recv()
-        at = lanes(y)
-        grad_out[:, at] = (both[:, at].astype(f32) + from_y[:, at].astype(f32)).astype(bf16)
-
+    for j in steps[3]:
+        pass_on(j)
     for c in c_t2_in:
         c.wait_recv()
     mine_t, other_t = tot.at[odd, half_piece(x)], tot.at[odd, half_piece(1 - x)]
@@ -378,31 +414,25 @@
     c_t1 = copy(k_t1, mine_t, mine_t, xpeer)
     c_t1_in = copy(k_t1, other_t, other_t, xpeer)
     c_t1.start()
-
-    @pl.when(away)
-    def _():
-        for j in range(chunks):
-            c_fin[j].wait_recv()
-            c_fin_y[j].start()
-
+    for j in steps[4]:
+        pass_on(j)
+    take(0, y)
+    for j in range(chunks // 2):
+        hand_over(j)
     c_t1_in.wait_recv()
     k_t0 = slots(1)
     c_t0 = copy(k_t0, tot.at[odd], tot.at[odd], mate)
     c_t0_in = copy(k_t0, tot.at[odd2], tot.at[odd2], mate)
     c_t0.start()
+    for j in range(chunks // 2, chunks):
+        hand_over(j)
+    take(1, y2)
 
     @pl.when(away)
     def _():
-        grad_out[:, lanes(y)] = fin[:, lanes(y)]
         for j in range(chunks):
             c_fin_y_in[j].wait_recv()
-            grad_out[:, lanes(y2, j)] = fin[:, lanes(y2, j)]
-
-    @pl.when(home)
-    def _():
-        c_home_in[1].wait_recv()
-        at = lanes(y2)
-        grad_out[:, at] = (both[:, at].astype(f32) + from_y[:, at].astype(f32)).astype(bf16)
+            grad_out[:, lanes(y2, j)] = fin[spot(y2, j)]
 
     c_t0_in.wait_recv()
     for side in range(2):
@@ -452,7 +482,7 @@
     deep = -(-width // grain) * grain
     half_rel = nrel // 2
     vmem = pl.BlockSpec(memory_space=pltpu.VMEM)
-    table = pltpu.VMEM((width, rows), bf16)
+    table = pltpu.VMEM((2 * chunks, width, rows // (2 * chunks)), bf16)
     spots = pltpu.VMEM((rows, slots // blocks), bf16)
     n_sems = 16 + 7 * chunks + n_dom
     params = dict(vmem_limit_bytes=56 * 1024 * 1024)

time: 62 us -> 63.4 us (1.023)
  Pallas kernels: 60.6 us -> 61.9 us
    pallas_call x1, Pallas kernels: 57.4 us -> 58.7 us  [local(): pl.pallas_call(functools.partial(kernel, n_dom, slots // blocks, neg_half...]
where the time goes in v5:
time: 63.4 us; the launch traced here: 63.2 us
  Pallas kernels  61.9 us (98%)
  between operations  1.29 us (2%)
    pallas_call x1, Pallas kernels, local(): pl.pallas_call(functools.partial(kernel, n_dom, slots // blocks, neg_half...  58.7 us
    pallas_call x1, Pallas kernels, local(): pl.pallas_call(update, grid=(rows // step,), out_shape=(jax.ShapeDtypeStr...  3.2 us

profile of v5, /device:TPU:24, one launch (start us, length us, event | category | flops | bytes accessed | tf_op | source)
XLA Modules:
  0.0 63.2 jit_solution(7153635492433082341)
XLA Ops:
  1.3 58.7 %shard_map.103 = (bf16[400,1024]{1,0:T(8,128)(2,1)}, f32[400,256]{1,0:T(8,128)}) custom-call(f32[400,1024]{1,0:T(8,128)} %bitcast.10, s32[2,1024]{1,0:T(2,128)} %ends_in.1, s32[1,1024]{1,0:T(1,128)} %bitcast.14, s32[2,512]{1,0:T(2,128)} %neg_in.1, s32[1,1]{1,0:T(1,128)} %bitcast.9.count_in, f32[400,256]{1,0:T(8,128)} %bitcast.12), custom_call_target="tpu_custom_call" | custom-call | tf_op jit(solution)/shard_map/pallas_call | solution.py:490
  60.0 3.2 %shard_map.104 = (f32[400,1024]{1,0:T(8,128)}, f32[1,1024]{1,0:T(1,128)}, f32[400,256]{1,0:T(8,128)}) custom-call(f32[400,1024]{1,0:T(8,128)} %bitcast.11, f32[1,1024]{1,0:T(1,128)} %bitcast.15, bf16[400,1024]{1,0:T(8,128)(2,1)} %get-tuple-element.8.grad, f32[400,256]{1,0:T(8,128)} %bitcast.13, f32[1,256]{1,0:T(1,128)} %bitcast.16, ...), custom_call_target="tpu_custom_call" | custom-call | tf_op jit(solution)/shard_map/pallas_call | solution.py:537

commit v6 on v4

--- a/solution.py
+++ b/solution.py
@@ -10,7 +10,7 @@
 entity_rate = 0.1
 relation_rate = 1.0
 MESH = pl.DeviceIdType.MESH
-STRIP = 64
+STRIP = 32
 f32, bf16 = jnp.float32, jnp.bfloat16
 
 
@@ -42,6 +42,7 @@
     count_in,
     rel,
     grad_out,
+    square_out,
     rel_out,
     ent_v,
     info_in,
@@ -56,18 +57,16 @@
     counts,
     fgb,
     from_mate,
-    both,
-    from_y,
     fin_send,
     fin,
+    square_send,
+    square,
     rg,
     rs0,
     r1,
     rs1,
     r2,
     rs2,
-    r3,
-    rs3,
     tot,
     ssem,
     rsem,
@@ -75,6 +74,7 @@
 ):
     width, rows = ent.shape
     nrel = rel.shape[1]
+    slot_count = ends_in.shape[1]
     half_rows = rows // 2
     chunk = half_rows // chunks
     d, b, y = lax.axis_index("dom"), lax.axis_index("bucket"), lax.axis_index("depth")
@@ -170,32 +170,33 @@
         c_info_home.wait()
 
     rel_at = lax.broadcasted_iota(jnp.int32, (nrel, 1), 0)
-    neg_lanes = pl.ds(pl.multiple_of(y * neg_half, neg_half), neg_half)
-    edge_lanes = pl.ds(pl.multiple_of(y * block, block), block)
-    left_ids = info[0, 0:1, edge_lanes]
-    right_ids = info[0, 1:2, edge_lanes]
-    rel_ids = info[0, 2:3, edge_lanes]
-    live = info[0, 3:4, edge_lanes]
-    slot_at = y * block + lax.broadcasted_iota(jnp.int32, (1, block), 1)
+    left_ids = info[0, 0:1]
+    right_ids = info[0, 1:2]
+    rel_ids = info[0, 2:3]
+    live = info[0, 3:4]
+    slot_at = lax.broadcasted_iota(jnp.int32, (1, slot_count), 1)
     active = (slot_at < live).astype(f32)
-    negs = jnp.concatenate([info[slot, 4:5, neg_lanes] for slot in range(2)], axis=1)
+    blocks = slot_count // block
 
     def strip(i):
         at = pl.ds(pl.multiple_of(i * STRIP, STRIP), STRIP)
         return at, i * STRIP + lax.broadcasted_iota(jnp.int32, (STRIP, 1), 0)
 
     def fold(value, join):
-        return join(value.reshape(STRIP // 8, 8, block), axis=0)
+        return join(value.reshape(STRIP // 8, 8, slot_count), axis=0)
 
     def spread(at):
-        return jnp.concatenate([counts[at, :]] * (block // 128), axis=1)
+        return jnp.concatenate([counts[c, at, :] for c in range(blocks) for _ in range(block // 128)], axis=1)
 
     def find(i, carry):
         at, row_at = strip(i)
-        hits = jnp.zeros((STRIP, 128), f32)
-        for t in range(2 * neg_half // 128):
-            hits += (row_at == negs[:, t * 128 : (t + 1) * 128]).astype(f32)
-        counts[at, :] = jnp.broadcast_to(jnp.sum(hits, axis=1, keepdims=True), (STRIP, 128))
+        for c in range(blocks):
+            hits = jnp.zeros((STRIP, 128), f32)
+            for slot in range(2):
+                for t in range(c * neg_half, (c + 1) * neg_half, 128):
+                    hits += (row_at == info[slot, 4:5, t : t + 128]).astype(f32)
+            found = jnp.sum(hits, axis=1, keepdims=True)
+            counts[c, at, :] = jnp.broadcast_to(found, (STRIP, 128))
         left_hot[at, :] = (row_at == left_ids).astype(bf16)
         return carry
 
@@ -236,7 +237,7 @@
             carry[1] + fold(jnp.where(row_at == right_ids, score, 0.0), jnp.sum),
         )
 
-    start = (jnp.full((8, block), -1e30, f32), jnp.zeros((8, block), f32))
+    start = (jnp.full((8, slot_count), -1e30, f32), jnp.zeros((8, slot_count), f32))
     best, hit = lax.fori_loop(0, rows // STRIP, largest, start)
     positive = jnp.sum(hit, axis=0, keepdims=True)
     peak = jnp.maximum(positive, jnp.max(best, axis=0, keepdims=True))
@@ -248,7 +249,7 @@
         scores[at, :] = shifted
         return carry + fold(count * shifted, jnp.sum)
 
-    total = lax.fori_loop(0, rows // STRIP, exponentials, jnp.zeros((8, block), f32))
+    total = lax.fori_loop(0, rows // STRIP, exponentials, jnp.zeros((8, slot_count), f32))
     pos_exp = jnp.exp(positive - peak)
     denom = pos_exp + jnp.sum(total, axis=0, keepdims=True)
     scale = active / denom
@@ -263,45 +264,51 @@
 
     lax.fori_loop(0, rows // STRIP, coefficients, 0)
 
-    k_far = slots(2)
-    c_far = []
-    for i, s in enumerate((y2, y)):
-        c_far.append(copy(k_far + i, fgb.at[:, lanes(s)], from_mate.at[:, lanes(s)], mate))
-        far_part = dot_nt(queries, high[lanes(s), :]) + dot_nt(queries, low[lanes(s), :])
-        fgb[:, lanes(s)] = far_part.astype(bf16)
-        c_far[i].start()
+    far_part = dot_nt(queries, high[lanes(y), :]) + dot_nt(queries, low[lanes(y), :])
+    c_far = move(slots(chunks), fgb, from_mate, y, mate)
+    for j in range(chunks):
+        fgb[:, lanes(y, j)] = far_part[:, j * chunk : (j + 1) * chunk]
+        c_far[j].start()
 
     query_grad = dot(far, high[...]) + dot(far, low[...])
-    own_terms = (query_grad * scaling).astype(bf16)
-
-    k_away = slots(chunks)
-    c_away = move(k_away, both, from_y, y2, ypeer)
-    c_away_in = move(k_away, both, from_y, y, ypeer)
-    k_home = slots(2)
-    c_home, c_home_in = [], []
-    for i, (s, o) in enumerate(((y2, y), (y, y2))):
-        c_home.append(copy(k_home + i, both.at[:, lanes(s)], from_y.at[:, lanes(s)], ypeer))
-        c_home_in.append(copy(k_home + i, both.at[:, lanes(o)], from_y.at[:, lanes(o)], ypeer))
+    own_part = dot_nt((query_grad * scaling).astype(bf16), left_hot[lanes(y), :])
+
     c_fin = move(slots(chunks), fin_send, fin, y, diag)
     k_fin_y = slots(chunks)
     c_fin_y = move(k_fin_y, fin, fin, y, ypeer)
     c_fin_y_in = move(k_fin_y, fin, fin, y2, ypeer)
-
-    def own_half(i, s):
-        own_part = dot_nt(own_terms, left_hot[lanes(s), :])
-        c_far[i].wait_recv()
-        both[:, lanes(s)] = (own_part + from_mate[:, lanes(s)].astype(f32)).astype(bf16)
+    for j in range(chunks):
+        at = lanes(y, j)
+        c_far[j].wait_recv()
+        sums = own_part[:, j * chunk : (j + 1) * chunk] + from_mate[:, at]
+
+        squares = jnp.broadcast_to(jnp.sum(sums * sums, axis=0, keepdims=True), (8, chunk))
 
         @pl.when(home)
         def _():
-            c_home[i].start()
-
-    own_half(0, y2)
+            square[:, at] = squares
+            fin[:, at] = sums.astype(bf16)
+            c_fin_y[j].start()
+
+        @pl.when(away)
+        def _():
+            square_send[:, at] = squares
+            fin_send[:, at] = sums.astype(bf16)
+            c_fin[j].start()
+
+    mine, other = square.at[:, lanes(y)], square.at[:, lanes(y2)]
+    c_square = copy(slots(1), square_send.at[:, lanes(y)], mine, diag)
+    k_square = slots(1)
+    c_square_y = copy(k_square, mine, mine, ypeer)
+    c_square_in = copy(k_square, other, other, ypeer)
+
+    @pl.when(home)
+    def _():
+        c_square_y.start()
 
     @pl.when(away)
     def _():
-        for c in c_away:
-            c.start()
+        c_square.start()
 
     rel_part = dot_nt(jnp.concatenate(parts_of(query_grad * left_rows, 2), axis=0), rel_hot)
     rel_part = rel_part[:width] + rel_part[width:]
@@ -312,8 +319,6 @@
     odd2 = 1 - odd
     c_r0 = copy(slots(1), rg.at[odd2], rs0, mate)
     c_r0.start()
-
-    own_half(1, y)
 
     half_deep = deep // 2
     part = half_deep // n_ring
@@ -341,21 +346,9 @@
     for c in c_r2:
         c.start()
 
-    @pl.when(away)
-    def _():
-        for j in range(chunks):
-            c_away_in[j].wait_recv()
-            at = lanes(y, j)
-            fin_send[:, at] = (both[:, at].astype(f32) + from_y[:, at].astype(f32)).astype(bf16)
-            c_fin[j].start()
-
     for c in c_r2:
         c.wait_recv()
-    r3[...] = r2[piece(0, lap), :] + jnp.sum(rs2[1:], axis=0)
-    c_r3 = copy(slots(1), r3, rs3, ypeer)
-    c_r3.start()
-    c_r3.wait_recv()
-    tot[odd, piece(x, lap), :] = r3[...] + rs3[...]
+    tot[odd, piece(x, lap), :] = r2[piece(0, lap), :] + jnp.sum(rs2[1:], axis=0)
     k_t2 = slots(n_ring)
     here = tot.at[odd, piece(x, lap)]
     c_t2, c_t2_in = [], []
@@ -365,12 +358,6 @@
         c_t2_in.append(copy(k_t2 + k, there, there, peers[k]))
         c_t2[-1].start()
 
-    @pl.when(home)
-    def _():
-        c_home_in[0].wait_recv()
-        at = lanes(y)
-        grad_out[:, at] = (both[:, at].astype(f32) + from_y[:, at].astype(f32)).astype(bf16)
-
     for c in c_t2_in:
         c.wait_recv()
     mine_t, other_t = tot.at[odd, half_piece(x)], tot.at[odd, half_piece(1 - x)]
@@ -381,6 +368,8 @@
 
     @pl.when(away)
     def _():
+        c_square.wait_recv()
+        c_square_y.start()
         for j in range(chunks):
             c_fin[j].wait_recv()
             c_fin_y[j].start()
@@ -391,50 +380,46 @@
     c_t0_in = copy(k_t0, tot.at[odd2], tot.at[odd2], mate)
     c_t0.start()
 
-    @pl.when(away)
-    def _():
-        grad_out[:, lanes(y)] = fin[:, lanes(y)]
-        for j in range(chunks):
-            c_fin_y_in[j].wait_recv()
-            grad_out[:, lanes(y2, j)] = fin[:, lanes(y2, j)]
-
-    @pl.when(home)
-    def _():
-        c_home_in[1].wait_recv()
-        at = lanes(y2)
-        grad_out[:, at] = (both[:, at].astype(f32) + from_y[:, at].astype(f32)).astype(bf16)
-
+    grad_out[:, lanes(y)] = fin[:, lanes(y)]
+    for j in range(chunks):
+        c_fin_y_in[j].wait_recv()
+        grad_out[:, lanes(y2, j)] = fin[:, lanes(y2, j)]
+
+    c_square_in.wait_recv()
+    square_out[...] = square[0:1]
     c_t0_in.wait_recv()
     for side in range(2):
         rel_out[:, side * (nrel // 2) : (side + 1) * (nrel // 2)] = tot[side, :width]
 
     @pl.when(home)
     def _():
-        for c in [c_left] + c_cross + c_mate0 + c_mate1 + c_home:
+        for c in [c_left] + c_cross + c_mate0 + c_mate1:
             c.wait_send()
 
     @pl.when(away)
     def _():
-        for c in c_stage + c_away + c_fin + c_fin_y:
+        for c in c_stage + c_fin + [c_square]:
             c.wait_send()
 
-    for c in [c_r0, c_r1, c_r3, c_t1, c_t0] + c_far + c_r2 + c_t2:
+    for c in [c_r0, c_r1, c_t1, c_t0, c_square_y] + c_far + c_fin_y + c_r2 + c_t2:
         c.wait_send()
 
 
-def adagrad(rate, values, state, grad, values_out, state_out):
-    updated = state[...] + jnp.sum(grad * grad, axis=0, keepdims=True) * (1.0 / grad.shape[0])
+def adagrad(rate, values, state, grad, squares, values_out, state_out):
+    updated = state[...] + squares * (1.0 / grad.shape[0])
     values_out[...] = values[...] - grad * (rate / jnp.sqrt(updated))
     if state_out is not None:
         state_out[...] = updated
 
 
-def update(ent, state, grad, rel, rel_state, rel_grad, ent_out, state_out, rel_out):
-    adagrad(entity_rate, ent, state, grad[...].astype(f32), ent_out, state_out)
+def update(ent, state, grad, squares, rel, rel_state, rel_grad, ent_out, state_out, rel_out):
+    adagrad(entity_rate, ent, state, grad[...].astype(f32), squares[...], ent_out, state_out)
 
     @pl.when(pl.program_id(0) == 0)
     def _():
-        adagrad(relation_rate, rel, rel_state, rel_grad[...], rel_out, None)
+        total = rel_grad[...]
+        rel_squares = jnp.sum(total * total, axis=0, keepdims=True)
+        adagrad(relation_rate, rel, rel_state, total, rel_squares, rel_out, None)
 
 
 def local(
@@ -453,18 +438,19 @@
     half_rel = nrel // 2
     vmem = pl.BlockSpec(memory_space=pltpu.VMEM)
     table = pltpu.VMEM((width, rows), bf16)
-    spots = pltpu.VMEM((rows, slots // blocks), bf16)
+    spots = pltpu.VMEM((rows, slots), bf16)
     n_sems = 16 + 7 * chunks + n_dom
     params = dict(vmem_limit_bytes=56 * 1024 * 1024)
     ent, rel = entities.T, relations.T
-    grad, rel_grad = pl.pallas_call(
+    grad, squares, rel_grad = pl.pallas_call(
         functools.partial(kernel, n_dom, slots // blocks, neg_half, chunks),
         out_shape=(
             jax.ShapeDtypeStruct((width, rows), bf16),
+            jax.ShapeDtypeStruct((1, rows), f32),
             jax.ShapeDtypeStruct((width, nrel), f32),
         ),
         in_specs=[pl.BlockSpec(memory_space=pl.ANY)] + [vmem] * 5,
-        out_specs=(vmem,) * 2,
+        out_specs=(vmem,) * 3,
         scratch_shapes=[
             pltpu.VMEM((width, rows), f32),
             pltpu.VMEM((8, slots), jnp.int32),
@@ -475,22 +461,20 @@
             spots,
             spots,
             spots,
-            pltpu.VMEM((rows, slots // blocks), f32),
-            pltpu.VMEM((rows, 128), f32),
+            pltpu.VMEM((rows, slots), f32),
+            pltpu.VMEM((blocks, rows, 128), f32),
+            pltpu.VMEM((width, rows), f32),
+            pltpu.VMEM((width, rows), f32),
             table,
             table,
-            table,
-            table,
-            table,
-            table,
+            pltpu.VMEM((8, rows), f32),
+            pltpu.VMEM((8, rows), f32),
             pltpu.VMEM((2, deep, half_rel), f32),
             pltpu.VMEM((deep, half_rel), f32),
             pltpu.VMEM((deep, half_rel), f32),
             pltpu.VMEM((deep // 2, half_rel), f32),
             pltpu.VMEM((deep // 2, half_rel), f32),
             pltpu.VMEM((n_dom // 2, deep // n_dom, half_rel), f32),
-            pltpu.VMEM((deep // n_dom, half_rel), f32),
-            pltpu.VMEM((deep // n_dom, half_rel), f32),
             pltpu.VMEM((2, deep, half_rel), f32),
             pltpu.SemaphoreType.DMA((n_sems,)),
             pltpu.SemaphoreType.DMA((n_sems,)),
@@ -512,10 +496,10 @@
             jax.ShapeDtypeStruct((1, rows), f32),
             jax.ShapeDtypeStruct((width, nrel), f32),
         ),
-        in_specs=[wide, line, wide, rel_all, pl.BlockSpec((1, nrel), lambda i: (0, 0)), rel_all],
+        in_specs=[wide, line, wide, line, rel_all, pl.BlockSpec((1, nrel), lambda i: (0, 0)), rel_all],
         out_specs=(wide, line, rel_all),
         compiler_params=pltpu.CompilerParams(**params),
-    )(ent, entity_state[None], grad, rel, relation_state[None], rel_grad)
+    )(ent, entity_state[None], grad, squares, rel, relation_state[None], rel_grad)
     return (new_ent.T, new_state[0], new_rel.T)
 
 

time: 62 us -> 63 us (1.016)
  Pallas kernels: 60.6 us -> 61.3 us
    pallas_call x1, Pallas kernels: 57.4 us -> 58.2 us  [local(): pl.pallas_call(functools.partial(kernel, n_dom, slots // blocks, neg_half...]
where the time goes in v6:
time: 63 us; the launch traced here: 62.6 us
  Pallas kernels  61.3 us (97%)
  between operations  1.29 us (2%)
    pallas_call x1, Pallas kernels, local(): pl.pallas_call(functools.partial(kernel, n_dom, slots // blocks, neg_half...  58.2 us
    pallas_call x1, Pallas kernels, local(): pl.pallas_call(update, grid=(rows // step,), out_shape=(jax.ShapeDtypeStr...  3.1 us

profile of v6, /device:TPU:24, one launch (start us, length us, event | category | flops | bytes accessed | tf_op | source)
XLA Modules:
  0.0 62.6 jit_solution(11348290395404962607)
XLA Ops:
  1.3 58.2 %shard_map.103 = (bf16[400,1024]{1,0:T(8,128)(2,1)}, f32[1,1024]{1,0:T(1,128)}, f32[400,256]{1,0:T(8,128)}) custom-call(f32[400,1024]{1,0:T(8,128)} %bitcast.10, s32[2,1024]{1,0:T(2,128)} %ends_in.1, s32[1,1024]{1,0:T(1,128)} %bitcast.14, s32[2,512]{1,0:T(2,128)} %neg_in.1, s32[1,1]{1,0:T(1,128)} %bitcast.9.count_in, f32[400,256]{1,0:T(8,128)} %bitcast.12), custom_call_target="tpu_custom_call" | custom-call | tf_op jit(solution)/shard_map/pallas_call | solution.py:445
  59.5 3.1 %shard_map.104 = (f32[400,1024]{1,0:T(8,128)}, f32[1,1024]{1,0:T(1,128)}, f32[400,256]{1,0:T(8,128)}) custom-call(f32[400,1024]{1,0:T(8,128)} %bitcast.11, f32[1,1024]{1,0:T(1,128)} %bitcast.15, bf16[400,1024]{1,0:T(8,128)(2,1)} %get-tuple-element.9.grad, f32[1,1024]{1,0:T(1,128)} %get-tuple-element.10.squares, f32[400,256]{1,0:T(8,128)} %bitcast.13, ...), custom_call_target="tpu_custom_call" | custom-call | tf_op jit(solution)/shard_map/pallas_call | solution.py:491
